TPU v7x, 32 devices: a whole 2x2x4 slice. The times are simulated.
32 devices in a mesh: fsdp: 8 (over z, x), tp: 4 (over y, core).
Axes of the slice: x: 2, y: 2, z: 4, core: 2. Of those that a mesh axis runs over, the one named last changes fastest.
Arguments:
- tokens: bfloat16 [2, 1024, 2048], P(None, 'fsdp'), may hold values from -6 to 6
- cotangent: bfloat16 [2, 1024, 2048], P(None, 'fsdp'), may hold values from -6 to 6
- expert_ids: int32 [2, 1024, 8], P(None, 'fsdp'), may hold values from 0 to 31, all different within a row; in each aligned block of 128 rows (0 to 127, 128 to 255, ..., all dimensions but the last counted through in order) at most 40 rows name the same one
- attention_gain: float32 [2048], replicated, may hold values from 0.5 to 1.5
- query_gain: float32 [128], replicated, may hold values from 0.5 to 1.5
- key_gain: float32 [128], replicated, may hold values from 0.5 to 1.5
- query_weight: bfloat16 [2048, 4096], P('fsdp', 'tp'), may hold values from -0.125 to 0.125
- key_weight: bfloat16 [2048, 512], P('fsdp', 'tp'), may hold values from -0.125 to 0.125
- value_weight: bfloat16 [2048, 512], P('fsdp', 'tp'), may hold values from -0.125 to 0.125
- output_weight: bfloat16 [2048, 4096], P('fsdp', 'tp'), may hold values from -0.75 to 0.75
- expert_gain: float32 [2048], replicated, may hold values from 0.5 to 1.5
- router_weight: bfloat16 [2048, 32], P('fsdp'), may hold values from -0.0625 to 0.0625
- gate_weight: bfloat16 [32, 768, 2048], P('fsdp', 'tp'), may hold values from -0.125 to 0.125
- up_weight: bfloat16 [32, 768, 2048], P('fsdp', 'tp'), may hold values from -0.125 to 0.125
- down_weight: bfloat16 [32, 768, 2048], P('fsdp', 'tp'), may hold values from -0.875 to 0.875
Outputs:
- layer_output: bfloat16 [2, 1024, 2048], P(None, 'fsdp')
- tokens_gradient: bfloat16 [2, 1024, 2048], P(None, 'fsdp')
- attention_gain_gradient: float32 [2048], P('fsdp')
- query_gain_gradient: float32 [128], P('fsdp')
- key_gain_gradient: float32 [128], P('fsdp')
- query_weight_gradient: float32 [2048, 4096], P('fsdp', 'tp')
- key_weight_gradient: float32 [2048, 512], P('fsdp', 'tp')
- value_weight_gradient: float32 [2048, 512], P('fsdp', 'tp')
- output_weight_gradient: float32 [2048, 4096], P('fsdp', 'tp')
- expert_gain_gradient: float32 [2048], P('fsdp')
- router_weight_gradient: float32 [2048, 32], P('fsdp')
- gate_weight_gradient: float32 [32, 768, 2048], P('fsdp', 'tp')
- up_weight_gradient: float32 [32, 768, 2048], P('fsdp', 'tp')
- down_weight_gradient: float32 [32, 768, 2048], P('fsdp', 'tp')
Inputs may be any that keep to these rules, and one draw needn't show every extreme that they name: `expert_ids`: each row names 8 different experts. Among the 128 tokens of one micro-batch on one index of fsdp (aligned blocks of 128 rows), no expert is named more than 40 times, and in some such block some expert is named exactly 40 times.
All inputs are finite; a program needn't handle non-finite values.
Results may differ from a plain program's by a relative error of at most 0.029.
Values may be sent and summed in bfloat16 or wider, within the bound.
A program may use at most 256 MiB of HBM per device.

v0:
```python
import math

import jax
import jax.numpy as jnp
from jax import lax
from jax.sharding import PartitionSpec as P

norm_eps = 1e-06
rope_base = 1000000.0
masked_score = -1e30


def rotate_half(values):
    middle = values.shape[-1] // 2
    return jnp.concatenate([-values[..., middle:], values[..., :middle]], axis=-1)


def rope_tables(positions, head_width):
    middle = head_width // 2
    frequency = rope_base ** (-jnp.arange(middle, dtype=jnp.float32) * 2.0 / head_width)
    angles = positions.astype(jnp.float32)[:, None] * frequency[None, :]
    angles = jnp.concatenate([angles, angles], axis=1)
    return (jnp.cos(angles), jnp.sin(angles))


def norm_parts(values):
    factor = lax.rsqrt(jnp.mean(values * values, axis=-1, keepdims=True) + norm_eps)
    return (values * factor, factor)


def norm_back(upstream, gain, normal, factor):
    scaled = upstream * gain
    return factor * (scaled - normal * jnp.mean(scaled * normal, axis=-1, keepdims=True))


def head_back(upstream, cosine_heads, sine_heads, gain, normal, factor):
    turned = upstream * cosine_heads - rotate_half(upstream * sine_heads)
    gain_part = jnp.sum(turned * normal, axis=(0, 1))
    return (norm_back(turned, gain, normal, factor), gain_part)


def fetch_weights(query_weight, key_weight, value_weight, output_weight, router_weight):
    return (
        lax.all_gather(query_weight, "fsdp", axis=0, tiled=True),
        lax.all_gather(key_weight, "fsdp", axis=0, tiled=True),
        lax.all_gather(value_weight, "fsdp", axis=0, tiled=True),
        lax.all_gather(output_weight, "fsdp", axis=0, tiled=True),
        lax.all_gather(router_weight, "fsdp", axis=0, tiled=True),
    )


def widen(summed):
    return lax.all_gather(summed, "tp", axis=3, tiled=True)


def carry_back(summed):
    return lax.all_to_all(summed, "fsdp", split_axis=0, concat_axis=0, tiled=True)


def send_home(summed):
    arrived_home = carry_back(widen(summed))
    return arrived_home


def per_device(
    tokens,
    cotangent,
    expert_ids,
    attention_gain,
    query_gain,
    key_gain,
    query_weight,
    key_weight,
    value_weight,
    output_weight,
    expert_gain,
    router_weight,
    gate_weight,
    up_weight,
    down_weight,
):
    micro_count = tokens.shape[0]
    tok_rows = tokens.shape[1]
    width = tokens.shape[2]
    route_count = expert_ids.shape[2]
    head_dim = query_gain.shape[0]
    local_heads = query_weight.shape[1] // head_dim
    local_groups = key_weight.shape[1] // head_dim
    group_size = local_heads // local_groups
    fsdp_count = lax.axis_size("fsdp")
    seq_len = tok_rows * fsdp_count
    experts_here = gate_weight.shape[0]
    expert_count = experts_here * fsdp_count
    capacity = max(2, 5 * tok_rows * route_count // (4 * expert_count))
    key_block = math.gcd(seq_len, 512)
    score_scale = 1.0 / math.sqrt(head_dim)
    query_count = tok_rows * group_size
    routed_total = tok_rows * route_count
    start_row = lax.axis_index("fsdp") * tok_rows
    positions = start_row + jnp.arange(tok_rows, dtype=jnp.int32)
    cosine_table, sine_table = rope_tables(positions, head_dim)
    cosine_heads = cosine_table[:, None, :]
    sine_heads = sine_table[:, None, :]
    query_pos = start_row + jnp.arange(query_count, dtype=jnp.int32) // group_size
    block_total = (start_row + tok_rows + key_block - 1) // key_block
    expert_range = jnp.arange(expert_count, dtype=jnp.int32)
    zero_row = jnp.zeros((1, width), jnp.bfloat16)

    def to_rows(tensor):
        return (
            tensor.reshape(tok_rows, local_groups, group_size, head_dim)
            .transpose(1, 0, 2, 3)
            .reshape(local_groups, query_count, head_dim)
        )

    def from_rows(tensor):
        return (
            tensor.reshape(local_groups, tok_rows, group_size, head_dim)
            .transpose(1, 0, 2, 3)
            .reshape(tok_rows, local_heads, head_dim)
        )

    acc_attention_gain = jnp.zeros((width,), jnp.float32)
    acc_head_gains = jnp.zeros((2, head_dim), jnp.float32)
    acc_query = jnp.zeros((width, local_heads * head_dim), jnp.float32)
    acc_key = jnp.zeros((width, local_groups * head_dim), jnp.float32)
    acc_value = jnp.zeros((width, local_groups * head_dim), jnp.float32)
    acc_output = jnp.zeros((width, local_heads * head_dim), jnp.float32)
    acc_expert_gain = jnp.zeros((width,), jnp.float32)
    acc_router = jnp.zeros((width, expert_count), jnp.float32)
    acc_gate = jnp.zeros(gate_weight.shape, jnp.float32)
    acc_up = jnp.zeros(up_weight.shape, jnp.float32)
    acc_down = jnp.zeros(down_weight.shape, jnp.float32)
    layer_rows = []
    input_rows = []
    for micro_index in range(micro_count):
        inputs = tokens[micro_index].astype(jnp.float32)
        query_full, key_full, value_full, output_full, router_full = fetch_weights(
            query_weight, key_weight, value_weight, output_weight, router_weight
        )
        input_hat, attention_factor = norm_parts(inputs)
        normed = (input_hat * attention_gain).astype(jnp.bfloat16)
        query_pre = jnp.dot(normed, query_full, preferred_element_type=jnp.float32).reshape(
            tok_rows, local_heads, head_dim
        )
        key_pre = jnp.dot(normed, key_full, preferred_element_type=jnp.float32).reshape(
            tok_rows, local_groups, head_dim
        )
        value_low = jnp.dot(normed, value_full, preferred_element_type=jnp.float32).astype(
            jnp.bfloat16
        )
        query_hat, query_factor = norm_parts(query_pre)
        key_hat, key_factor = norm_parts(key_pre)
        query_scaled = query_hat * query_gain
        key_scaled = key_hat * key_gain
        query_low = (query_scaled * cosine_heads + rotate_half(query_scaled) * sine_heads).astype(
            jnp.bfloat16
        )
        key_low = (key_scaled * cosine_heads + rotate_half(key_scaled) * sine_heads).astype(
            jnp.bfloat16
        )
        key_all, value_all = (
            lax.all_gather(
                key_low.reshape(tok_rows, local_groups * head_dim), "fsdp", axis=0, tiled=True
            ),
            lax.all_gather(value_low, "fsdp", axis=0, tiled=True),
        )
        key_heads = key_all.reshape(seq_len, local_groups, head_dim).transpose(1, 0, 2)
        value_heads = value_all.reshape(seq_len, local_groups, head_dim).transpose(1, 0, 2)
        query_rows = to_rows(query_low)

        def scores_at(block_index):
            block_start = block_index * key_block
            key_slice = lax.dynamic_slice_in_dim(key_heads, block_start, key_block, 1)
            raw_scores = (
                jnp.einsum(
                    "gqd,gkd->gqk", query_rows, key_slice, preferred_element_type=jnp.float32
                )
                * score_scale
            )
            allowed = (block_start + jnp.arange(key_block, dtype=jnp.int32))[None, :] <= query_pos[
                :, None
            ]
            return (jnp.where(allowed[None], raw_scores, masked_score), allowed, block_start)

        def stats_step(block_index, carried):
            run_peak, run_total = carried
            scores, allowed, block_start = scores_at(block_index)
            new_peak = jnp.maximum(run_peak, jnp.max(scores, axis=-1))
            terms = jnp.where(allowed[None], jnp.exp(scores - new_peak[..., None]), 0.0)
            return (new_peak, run_total * jnp.exp(run_peak - new_peak) + jnp.sum(terms, axis=-1))

        start_stats = (
            jnp.full((local_groups, query_count), masked_score, jnp.float32),
            jnp.zeros((local_groups, query_count), jnp.float32),
        )
        run_peak, run_total = lax.fori_loop(0, block_total, stats_step, start_stats)
        log_total = run_peak + jnp.log(run_total)

        def value_step(block_index, acc_context):
            scores, allowed, block_start = scores_at(block_index)
            probs_low = jnp.where(
                allowed[None], jnp.exp(scores - log_total[..., None]), 0.0
            ).astype(jnp.bfloat16)
            value_slice = lax.dynamic_slice_in_dim(value_heads, block_start, key_block, 1)
            return acc_context + jnp.einsum(
                "gqk,gkd->gqd", probs_low, value_slice, preferred_element_type=jnp.float32
            )

        context_rows = lax.fori_loop(
            0,
            block_total,
            value_step,
            jnp.zeros((local_groups, query_count, head_dim), jnp.float32),
        )
        context_low = (
            from_rows(context_rows).reshape(tok_rows, local_heads * head_dim).astype(jnp.bfloat16)
        )
        branch_part = jnp.einsum(
            "th,dh->td", context_low, output_full, preferred_element_type=jnp.float32
        )
        resid = inputs + lax.psum(branch_part.astype(jnp.bfloat16), "tp").astype(jnp.float32)
        resid_hat, expert_factor = norm_parts(resid)
        expert_in = (resid_hat * expert_gain).astype(jnp.bfloat16)
        logits = jnp.dot(expert_in, router_full, preferred_element_type=jnp.float32)
        routes_now = expert_ids[micro_index]
        choose = (routes_now[:, :, None] == expert_range[None, None, :]).astype(jnp.float32)
        picked = jnp.sum(choose * logits[:, None, :], axis=-1)
        shifted = jnp.exp(picked - jnp.max(picked, axis=-1, keepdims=True))
        gate_probs = shifted / jnp.sum(shifted, axis=-1, keepdims=True)
        flat_routes = routes_now.reshape(-1)
        onehot = (flat_routes[:, None] == expert_range[None, :]).astype(jnp.int32)
        rank_in = jnp.sum((jnp.cumsum(onehot, axis=0) - onehot) * onehot, axis=1)
        slot_index = flat_routes * capacity + rank_in
        slot_source = (
            jnp.full((expert_count * capacity,), routed_total, jnp.int32)
            .at[slot_index]
            .set(jnp.arange(routed_total, dtype=jnp.int32))
        )
        padded_in = jnp.concatenate([expert_in, zero_row], axis=0)
        outgoing = padded_in[slot_source // route_count].reshape(
            fsdp_count, experts_here, capacity, width
        )
        arrived = lax.all_to_all(outgoing, "fsdp", split_axis=0, concat_axis=0, tiled=True)
        gate_pre = jnp.einsum(
            "secd,efd->secf", arrived, gate_weight, preferred_element_type=jnp.float32
        )
        up_pre = jnp.einsum(
            "secd,efd->secf", arrived, up_weight, preferred_element_type=jnp.float32
        )
        gate_sigmoid = jax.nn.sigmoid(gate_pre)
        inner_low = (gate_pre * gate_sigmoid * up_pre).astype(jnp.bfloat16)
        result_part = jnp.einsum(
            "secf,efd->secd", inner_low, down_weight, preferred_element_type=jnp.float32
        )
        result_low = lax.psum_scatter(
            result_part.astype(jnp.bfloat16), "tp", scatter_dimension=3, tiled=True
        )
        result_home = send_home(result_low)
        routed = (
            result_home.reshape(expert_count * capacity, width)[slot_index]
            .astype(jnp.float32)
            .reshape(tok_rows, route_count, width)
        )
        layer_rows.append(
            (resid + jnp.sum(gate_probs[:, :, None] * routed, axis=1)).astype(jnp.bfloat16)
        )
        query_full, key_full, value_full, output_full, router_full = fetch_weights(
            query_weight, key_weight, value_weight, output_weight, router_weight
        )
        out_grad = cotangent[micro_index].astype(jnp.float32)
        d_route = (
            (gate_probs[:, :, None] * out_grad[:, None, :])
            .astype(jnp.bfloat16)
            .reshape(routed_total, width)
        )
        d_gate_probs = jnp.sum(out_grad[:, None, :] * routed, axis=-1)
        d_pick = gate_probs * (
            d_gate_probs - jnp.sum(gate_probs * d_gate_probs, axis=-1, keepdims=True)
        )
        d_logits = jnp.sum(choose * d_pick[:, :, None], axis=1).astype(jnp.bfloat16)
        grad_outgoing = jnp.concatenate([d_route, zero_row], axis=0)[slot_source].reshape(
            fsdp_count, experts_here, capacity, width
        )
        grad_arrived = lax.all_to_all(
            grad_outgoing, "fsdp", split_axis=0, concat_axis=0, tiled=True
        )
        d_inner = jnp.einsum(
            "secd,efd->secf", grad_arrived, down_weight, preferred_element_type=jnp.float32
        )
        acc_down = acc_down + jnp.einsum(
            "secf,secd->efd", inner_low, grad_arrived, preferred_element_type=jnp.float32
        )
        d_gate_low = (
            d_inner * up_pre * gate_sigmoid * (1.0 + gate_pre * (1.0 - gate_sigmoid))
        ).astype(jnp.bfloat16)
        d_up_low = (d_inner * gate_pre * gate_sigmoid).astype(jnp.bfloat16)
        acc_gate = acc_gate + jnp.einsum(
            "secf,secd->efd", d_gate_low, arrived, preferred_element_type=jnp.float32
        )
        acc_up = acc_up + jnp.einsum(
            "secf,secd->efd", d_up_low, arrived, preferred_element_type=jnp.float32
        )
        d_copy_part = jnp.einsum(
            "secf,efd->secd", d_gate_low, gate_weight, preferred_element_type=jnp.float32
        ) + jnp.einsum("secf,efd->secd", d_up_low, up_weight, preferred_element_type=jnp.float32)
        d_copy_low = lax.psum_scatter(
            d_copy_part.astype(jnp.bfloat16), "tp", scatter_dimension=3, tiled=True
        )
        d_copy_home = send_home(d_copy_low)
        d_copies = (
            d_copy_home.reshape(expert_count * capacity, width)[slot_index]
            .astype(jnp.float32)
            .reshape(tok_rows, route_count, width)
        )
        d_expert_in = jnp.sum(d_copies, axis=1) + jnp.dot(
            d_logits, router_full.T, preferred_element_type=jnp.float32
        )
        acc_router = acc_router + jnp.dot(expert_in.T, d_logits, preferred_element_type=jnp.float32)
        acc_expert_gain = acc_expert_gain + jnp.sum(d_expert_in * resid_hat, axis=0)
        d_resid = out_grad + norm_back(d_expert_in, expert_gain, resid_hat, expert_factor)
        d_branch = d_resid.astype(jnp.bfloat16)
        acc_output = acc_output + jnp.einsum(
            "td,th->dh", d_branch, context_low, preferred_element_type=jnp.float32
        )
        d_context = jnp.dot(d_branch, output_full, preferred_element_type=jnp.float32).astype(
            jnp.bfloat16
        )
        d_context_rows = to_rows(d_context.reshape(tok_rows, local_heads, head_dim))
        delta_rows = jnp.sum(d_context_rows.astype(jnp.float32) * context_rows, axis=-1)

        def grad_step(block_index, carried):
            d_query_rows, key_grads_all = carried
            scores, allowed, block_start = scores_at(block_index)
            probs = jnp.where(allowed[None], jnp.exp(scores - log_total[..., None]), 0.0)
            key_slice = lax.dynamic_slice_in_dim(key_heads, block_start, key_block, 1)
            value_slice = lax.dynamic_slice_in_dim(value_heads, block_start, key_block, 1)
            d_probs = jnp.einsum(
                "gqd,gkd->gqk", d_context_rows, value_slice, preferred_element_type=jnp.float32
            )
            d_scores = (probs * (d_probs - delta_rows[..., None])).astype(jnp.bfloat16)
            d_query_rows = (
                d_query_rows
                + jnp.einsum(
                    "gqk,gkd->gqd", d_scores, key_slice, preferred_element_type=jnp.float32
                )
                * score_scale
            )
            d_key_block = (
                jnp.einsum("gqk,gqd->kgd", d_scores, query_rows, preferred_element_type=jnp.float32)
                * score_scale
            )
            d_value_block = jnp.einsum(
                "gqk,gqd->kgd",
                probs.astype(jnp.bfloat16),
                d_context_rows,
                preferred_element_type=jnp.float32,
            )
            current = lax.dynamic_slice_in_dim(key_grads_all, block_start, key_block, 0)
            updated = current + jnp.concatenate([d_key_block, d_value_block], axis=-1)
            return (
                d_query_rows,
                lax.dynamic_update_slice_in_dim(key_grads_all, updated, block_start, 0),
            )

        start_grads = (
            jnp.zeros((local_groups, query_count, head_dim), jnp.float32),
            jnp.zeros((seq_len, local_groups, 2 * head_dim), jnp.float32),
        )
        d_query_rows, key_grads_all = lax.fori_loop(0, block_total, grad_step, start_grads)
        key_grads = (
            lax.psum_scatter(
                key_grads_all.reshape(seq_len, local_groups * 2 * head_dim).astype(jnp.bfloat16),
                "fsdp",
                scatter_dimension=0,
                tiled=True,
            )
            .astype(jnp.float32)
            .reshape(tok_rows, local_groups, 2 * head_dim)
        )
        d_value_low = (
            key_grads[..., head_dim:]
            .reshape(tok_rows, local_groups * head_dim)
            .astype(jnp.bfloat16)
        )
        d_key_pre, key_gain_part = head_back(
            key_grads[..., :head_dim], cosine_heads, sine_heads, key_gain, key_hat, key_factor
        )
        d_query_pre, query_gain_part = head_back(
            from_rows(d_query_rows), cosine_heads, sine_heads, query_gain, query_hat, query_factor
        )
        d_query_low = d_query_pre.astype(jnp.bfloat16).reshape(tok_rows, local_heads * head_dim)
        d_key_low = d_key_pre.astype(jnp.bfloat16).reshape(tok_rows, local_groups * head_dim)
        d_normed_part = jnp.dot(d_query_low, query_full.T, preferred_element_type=jnp.float32)
        d_normed_part = d_normed_part + jnp.dot(
            d_key_low, key_full.T, preferred_element_type=jnp.float32
        )
        d_normed_part = d_normed_part + jnp.dot(
            d_value_low, value_full.T, preferred_element_type=jnp.float32
        )
        acc_query = acc_query + jnp.dot(normed.T, d_query_low, preferred_element_type=jnp.float32)
        acc_key = acc_key + jnp.dot(normed.T, d_key_low, preferred_element_type=jnp.float32)
        acc_value = acc_value + jnp.dot(normed.T, d_value_low, preferred_element_type=jnp.float32)
        d_normed, head_gain_parts = (
            lax.psum(d_normed_part.astype(jnp.bfloat16), "tp").astype(jnp.float32),
            lax.psum(jnp.stack([query_gain_part, key_gain_part]).astype(jnp.bfloat16), "tp").astype(
                jnp.float32
            ),
        )
        acc_head_gains = acc_head_gains + head_gain_parts
        acc_attention_gain = acc_attention_gain + jnp.sum(d_normed * input_hat, axis=0)
        input_rows.append(
            (d_resid + norm_back(d_normed, attention_gain, input_hat, attention_factor)).astype(
                jnp.bfloat16
            )
        )
    summed = (
        lax.psum_scatter(
            acc_attention_gain.astype(jnp.bfloat16), "fsdp", scatter_dimension=0, tiled=True
        ).astype(jnp.float32),
        lax.psum_scatter(
            acc_head_gains[0].astype(jnp.bfloat16), "fsdp", scatter_dimension=0, tiled=True
        ).astype(jnp.float32),
        lax.psum_scatter(
            acc_head_gains[1].astype(jnp.bfloat16), "fsdp", scatter_dimension=0, tiled=True
        ).astype(jnp.float32),
        lax.psum_scatter(
            acc_query.astype(jnp.bfloat16), "fsdp", scatter_dimension=0, tiled=True
        ).astype(jnp.float32),
        lax.psum_scatter(
            acc_key.astype(jnp.bfloat16), "fsdp", scatter_dimension=0, tiled=True
        ).astype(jnp.float32),
        lax.psum_scatter(
            acc_value.astype(jnp.bfloat16), "fsdp", scatter_dimension=0, tiled=True
        ).astype(jnp.float32),
        lax.psum_scatter(
            acc_output.astype(jnp.bfloat16), "fsdp", scatter_dimension=0, tiled=True
        ).astype(jnp.float32),
        lax.psum_scatter(
            acc_expert_gain.astype(jnp.bfloat16), "fsdp", scatter_dimension=0, tiled=True
        ).astype(jnp.float32),
        lax.psum_scatter(
            acc_router.astype(jnp.bfloat16), "fsdp", scatter_dimension=0, tiled=True
        ).astype(jnp.float32),
    )
    return (
        jnp.stack(layer_rows),
        jnp.stack(input_rows),
        summed[0],
        summed[1],
        summed[2],
        summed[3],
        summed[4],
        summed[5],
        summed[6],
        summed[7],
        summed[8],
        acc_gate,
        acc_up,
        acc_down,
    )


def solution(mesh):
    return jax.shard_map(
        per_device,
        mesh=mesh,
        in_specs=(
            P(None, "fsdp", None),
            P(None, "fsdp", None),
            P(None, "fsdp", None),
            P(),
            P(),
            P(),
            P("fsdp", "tp"),
            P("fsdp", "tp"),
            P("fsdp", "tp"),
            P("fsdp", "tp"),
            P(),
            P("fsdp", None),
            P("fsdp", "tp", None),
            P("fsdp", "tp", None),
            P("fsdp", "tp", None),
        ),
        out_specs=(
            P(None, "fsdp", None),
            P(None, "fsdp", None),
            P("fsdp"),
            P("fsdp"),
            P("fsdp"),
            P("fsdp", "tp"),
            P("fsdp", "tp"),
            P("fsdp", "tp"),
            P("fsdp", "tp"),
            P("fsdp"),
            P("fsdp", None),
            P("fsdp", "tp", None),
            P("fsdp", "tp", None),
            P("fsdp", "tp", None),
        ),
        check_vma=False,
    )
```

profile of v0, /device:TPU:16, one launch (start us, length us, event | category | flops | bytes accessed | tf_op | source)
XLA Modules:
  0.0 2022.7 jit_solution(7814428608988766456)
XLA Ops:
  10.4 28.4 %all_gather.26 = bf16[2048,128]{1,0:T(8,128)(2,1)S(1)} all-gather(bf16[256,128]{1,0:T(8,128)(2,1)} %param.34), channel_id=1, replica_groups=mesh['fsdp'=8,'tp'=4] {'fsdp'}, dimensions={0}, use_global_device_ids=true | all-gather | bytes 589824 | tf_op jit(solution)/shard_map/all_gather | solution.py:45
  42.0 33.7 %all_gather.57 = bf16[2048,128]{1,0:T(8,128)(2,1)S(1)} all-gather(bf16[256,128]{1,0:T(8,128)(2,1)S(1)} %copy-done.94), channel_id=1, replica_groups=mesh['fsdp'=8,'tp'=4] {'fsdp'}, dimensions={0}, use_global_device_ids=true | all-gather | bytes 589824 | tf_op jit(solution)/shard_map/all_gather | solution.py:46
  80.1 29.2 %all_gather.27 = bf16[1024,128]{0,1:T(8,128)(2,1)S(1)} all-gather(bf16[128,128]{0,1:T(8,128)(2,1)S(1)} %get-tuple-element.886), channel_id=1, replica_groups=mesh['fsdp'=8,'tp'=4] {'fsdp'}, dimensions={0}, use_global_device_ids=true | all-gather | bytes 294912 | tf_op jit(solution)/shard_map/all_gather | solution.py:163
  110.2 29.6 %all_gather.58 = bf16[1024,128]{1,0:T(8,128)(2,1)S(1)} all-gather(bf16[128,128]{1,0:T(8,128)(2,1)S(1)} %convolution_convert_fusion.5), channel_id=1, replica_groups=mesh['fsdp'=8,'tp'=4] {'fsdp'}, dimensions={0}, use_global_device_ids=true | all-gather | bytes 294912 | tf_op jit(solution)/shard_map/all_gather | solution.py:166
  139.7 32.4 %all_gather.62 = bf16[1024,128]{0,1:T(8,128)(2,1)} all-gather(bf16[128,128]{0,1:T(8,128)(2,1)S(1)} %get-tuple-element.887), channel_id=1, replica_groups=mesh['fsdp'=8,'tp'=4] {'fsdp'}, dimensions={0}, use_global_device_ids=true | all-gather | bytes 294912 | tf_op jit(solution)/shard_map/all_gather | solution.py:163
  173.9 29.2 %all_gather.63 = bf16[1024,128]{1,0:T(8,128)(2,1)} all-gather(bf16[128,128]{1,0:T(8,128)(2,1)S(1)} %convolution_convert_fusion.4), channel_id=1, replica_groups=mesh['fsdp'=8,'tp'=4] {'fsdp'}, dimensions={0}, use_global_device_ids=true | all-gather | bytes 294912 | tf_op jit(solution)/shard_map/all_gather | solution.py:166
  370.9 98.2 %all-to-all-done.4 = bf16[8,4,40,2048]{3,2,1,0:T(8,128)(2,1)} async-done(((bf16[8,4,40,2048]{3,2,1,0:T(8,128)(2,1)}), bf16[8,4,40,2048]{3,2,1,0:T(8,128)(2,1)}, u32[]{:S(2)}, u32[]{:S(2)}) %all-to-all-start.4) | async-done | bytes 5242912 | tf_op jit(solution)/shard_map/all_to_all | solution.py:285
  515.7 83.5 %all-to-all-done = bf16[8,4,40,2048]{3,2,1,0:T(8,128)(2,1)} async-done(((bf16[8,4,40,2048]{3,2,1,0:T(8,128)(2,1)}), bf16[8,4,40,2048]{3,2,1,0:T(8,128)(2,1)}, u32[]{:S(2)}, u32[]{:S(2)}) %all-to-all-start) | async-done | bytes 5242912 | tf_op jit(solution)/shard_map/all_to_all | solution.py:244
  642.3 76.4 %all-to-all-done.2 = bf16[8,4,40,2048]{3,2,1,0:T(8,128)(2,1)} async-done(((bf16[8,4,40,2048]{3,2,1,0:T(8,128)(2,1)}), bf16[8,4,40,2048]{3,2,1,0:T(8,128)(2,1)}, u32[]{:S(2)}, u32[]{:S(2)}) %all-to-all-start.2) | async-done | bytes 5242912 | tf_op jit(solution)/shard_map/all_to_all | solution.py:244
  744.0 94.3 %all-to-all-done.6 = bf16[8,4,40,2048]{3,2,1,0:T(8,128)(2,1)} async-done(((bf16[8,4,40,2048]{3,2,1,0:T(8,128)(2,1)}), bf16[8,4,40,2048]{3,2,1,0:T(8,128)(2,1)}, u32[]{:S(2)}, u32[]{:S(2)}) %all-to-all-start.6) | async-done | bytes 5242912 | tf_op jit(solution)/shard_map/all_to_all | solution.py:285
  858.3 44.1 %reduce-scatter.18.cloned.1.call-done = bf16[8,4,40,512]{3,2,0,1:T(8,128)(2,1)} async-done(((bf16[8,4,40,2048]{3,2,0,1:T(8,128)(2,1)}), bf16[8,4,40,512]{3,2,0,1:T(8,128)(2,1)}) %reduce-scatter.18.cloned.1.call-update) | async-done | bytes 1310736 | tf_op jit(solution)/shard_map/reduce_scatter | solution.py:256
  902.4 41.9 %all-gather.11.cloned.1.call-done = bf16[8,4,40,2048]{3,2,0,1:T(8,128)(2,1)} async-done(((bf16[8,4,40,512]{3,2,0,1:T(8,128)(2,1)}), bf16[8,4,40,2048]{3,2,0,1:T(8,128)(2,1)}) %all-gather.11.cloned.1.call-update) | async-done | bytes 5242896 | tf_op jit(solution)/shard_map/all_gather | solution.py:53
  956.1 43.0 %reduce-scatter.20.cloned.1.call-done = bf16[8,4,40,512]{3,2,0,1:T(8,128)(2,1)} async-done(((bf16[8,4,40,2048]{3,2,0,1:T(8,128)(2,1)}), bf16[8,4,40,512]{3,2,0,1:T(8,128)(2,1)}) %reduce-scatter.20.cloned.1.call-update) | async-done | bytes 1310736 | tf_op jit(solution)/shard_map/reduce_scatter | solution.py:307
  1005.9 35.2 %all-gather.13.cloned.1.call-done = bf16[8,4,40,2048]{3,2,0,1:T(8,128)(2,1)} async-done(((bf16[8,4,40,512]{3,2,0,1:T(8,128)(2,1)}), bf16[8,4,40,2048]{3,2,0,1:T(8,128)(2,1)}) %all-gather.13.cloned.1.call-update) | async-done | bytes 5242896 | tf_op jit(solution)/shard_map/all_gather | solution.py:53
  1088.8 100.0 %all-to-all-done.3 = bf16[8,4,40,2048]{3,2,1,0:T(8,128)(2,1)} async-done(((bf16[8,4,40,2048]{3,2,1,0:T(8,128)(2,1)}), bf16[8,4,40,2048]{3,2,1,0:T(8,128)(2,1)}, u32[]{:S(2)}, u32[]{:S(2)}) %all-to-all-start.3) | async-done | bytes 5242912 | tf_op jit(solution)/shard_map/all_to_all | solution.py:57
  1197.4 42.2 %all-gather.17.cloned.1.call-done = bf16[8,4,40,2048]{3,2,0,1:T(8,128)(2,1)} async-done(((bf16[8,4,40,512]{3,2,0,1:T(8,128)(2,1)}), bf16[8,4,40,2048]{3,2,0,1:T(8,128)(2,1)}) %all-gather.17.cloned.1.call-update) | async-done | bytes 5242896 | tf_op jit(solution)/shard_map/all_gather | solution.py:53
  1245.3 63.0 %all-to-all-done.5 = bf16[8,4,40,2048]{3,2,1,0:T(8,128)(2,1)} async-done(((bf16[8,4,40,2048]{3,2,1,0:T(8,128)(2,1)}), bf16[8,4,40,2048]{3,2,1,0:T(8,128)(2,1)}, u32[]{:S(2)}, u32[]{:S(2)}) %all-to-all-start.5) | async-done | bytes 5242912 | tf_op jit(solution)/shard_map/all_to_all | solution.py:57
  1370.7 57.2 %all-to-all-done.7 = bf16[8,4,40,2048]{3,2,1,0:T(8,128)(2,1)} async-done(((bf16[8,4,40,2048]{3,2,1,0:T(8,128)(2,1)}), bf16[8,4,40,2048]{3,2,1,0:T(8,128)(2,1)}, u32[]{:S(2)}, u32[]{:S(2)}) %all-to-all-start.7) | async-done | bytes 5242912 | tf_op jit(solution)/shard_map/all_to_all | solution.py:57
  1534.0 63.9 %reduce-scatter.34.cloned.1.call-done = bf16[128,256]{1,0:T(8,128)(2,1)} async-done(((bf16[1024,256]{1,0:T(8,128)(2,1)}), bf16[128,256]{1,0:T(8,128)(2,1)}) %reduce-scatter.34.cloned.1.call-update) | async-done | bytes 65552
  1669.5 32.2 %all-reduce.15.cloned.1.call-done = (bf16[128,2048]{1,0:T(8,128)(2,1)}, bf16[128,2048]{1,0:T(8,128)(2,1)}) async-done(((bf16[128,2048]{1,0:T(8,128)(2,1)}, bf16[128,2048]{1,0:T(8,128)(2,1)}), (bf16[128,2048]{1,0:T(8,128)(2,1)}, bf16[128,2048]{1,0:T(8,128)(2,1)})) %all-reduce.15.cloned.1.call-update) | async-done | bytes 1048592 | tf_op jit(solution)/shard_map/psum | solution.py:405
  1726.8 39.4 %reduce-scatter.28.cloned.1.call-done = bf16[256,128]{1,0:T(8,128)(2,1)} async-done(((bf16[2048,128]{1,0:T(8,128)(2,1)}), bf16[256,128]{1,0:T(8,128)(2,1)}) %reduce-scatter.28.cloned.1.call-update) | async-done | bytes 65552 | tf_op jit(solution)/shard_map/reduce_scatter | solution.py:433
  1767.7 63.0 %reduce-scatter.26.cloned.1.call-done = bf16[256,128]{1,0:T(8,128)(2,1)} async-done(((bf16[2048,128]{1,0:T(8,128)(2,1)}), bf16[256,128]{1,0:T(8,128)(2,1)}) %reduce-scatter.26.cloned.1.call-update) | async-done | bytes 65552 | tf_op jit(solution)/shard_map/reduce_scatter | solution.py:430
  1832.2 89.8 %reduce-scatter.30.cloned.1.call-done = bf16[256,1024]{1,0:T(8,128)(2,1)} async-done(((bf16[2048,1024]{1,0:T(8,128)(2,1)}), bf16[256,1024]{1,0:T(8,128)(2,1)}) %reduce-scatter.30.cloned.1.call-update) | async-done | bytes 524304 | tf_op jit(solution)/shard_map/reduce_scatter | solution.py:436
  1924.2 89.7 %reduce-scatter.24.cloned.1.call-done = bf16[256,1024]{1,0:T(8,128)(2,1)} async-done(((bf16[2048,1024]{1,0:T(8,128)(2,1)}), bf16[256,1024]{1,0:T(8,128)(2,1)}) %reduce-scatter.24.cloned.1.call-update) | async-done | bytes 524304 | tf_op jit(solution)/shard_map/reduce_scatter | solution.py:427
  (656 shorter events, 717.0 us)
Async XLA Ops:
  7.2 226.3 %all-gather.7.cloned.1.call-start = ((), (), s32[]{:S(2)}) async-start(), calls=%async_computation.19 | async-start | bytes 4718592 | tf_op jit(solution)/shard_map/all_gather | solution.py:44
  8.0 273.3 %all-gather.9.cloned.1.call-start = ((), (), s32[]{:S(2)}) async-start(), calls=%async_computation.20 | async-start | bytes 4718592 | tf_op jit(solution)/shard_map/all_gather | solution.py:47
  8.7 317.5 %all-reduce.17.cloned.1.call-start = ((), (), s32[]{:S(2)}) async-start(), calls=%async_computation.37 | async-start | bytes 2097152 | tf_op jit(solution)/shard_map/psum | solution.py:222
  469.2 130.0 %all-to-all-start = ((bf16[8,4,40,2048]{3,2,1,0:T(8,128)(2,1)}), bf16[8,4,40,2048]{3,2,1,0:T(8,128)(2,1)}, u32[]{:S(2)}, u32[]{:S(2)}) async-start(bf16[8,4,40,2048]{3,2,1,0:T(8,128)(2,1)} %bitcast.743), calls=%async_computation | async-start | bytes 10485760 | tf_op jit(solution)/shard_map/all_to_all | solution.py:244
  599.2 119.6 %all-to-all-start.2 = ((bf16[8,4,40,2048]{3,2,1,0:T(8,128)(2,1)}), bf16[8,4,40,2048]{3,2,1,0:T(8,128)(2,1)}, u32[]{:S(2)}, u32[]{:S(2)}) async-start(bf16[8,4,40,2048]{3,2,1,0:T(8,128)(2,1)} %bitcast.744), calls=%async_computation.3 | async-start | bytes 10485760 | tf_op jit(solution)/shard_map/all_to_all | solution.py:244
  718.8 119.6 %all-to-all-start.6 = ((bf16[8,4,40,2048]{3,2,1,0:T(8,128)(2,1)}), bf16[8,4,40,2048]{3,2,1,0:T(8,128)(2,1)}, u32[]{:S(2)}, u32[]{:S(2)}) async-start(bf16[8,4,40,2048]{3,2,1,0:T(8,128)(2,1)} %bitcast.745), calls=%async_computation.9 | async-start | bytes 10485760 | tf_op jit(solution)/shard_map/all_to_all | solution.py:285
  726.7 122.8 %reduce-scatter.16.cloned.1.call-start = ((), (), s32[]{:S(2)}) async-start(), calls=%async_computation.21 | async-start | bytes 6553600 | tf_op jit(solution)/shard_map/reduce_scatter | solution.py:256
  731.7 170.7 %reduce-scatter.18.cloned.1.call-start = ((), (), s32[]{:S(2)}) async-start(), calls=%async_computation.23 | async-start | bytes 6553600 | tf_op jit(solution)/shard_map/reduce_scatter | solution.py:256
  850.0 149.1 %reduce-scatter.20.cloned.1.call-start = ((), (), s32[]{:S(2)}) async-start(), calls=%async_computation.25 | async-start | bytes 6553600 | tf_op jit(solution)/shard_map/reduce_scatter | solution.py:307
  858.3 182.8 %all-gather.13.cloned.1.call-start = ((), (), s32[]{:S(2)}) async-start(), calls=%async_computation.24 | async-start | bytes 6553600 | tf_op jit(solution)/shard_map/all_gather | solution.py:53
  950.1 118.8 %all-to-all-start.1 = ((bf16[8,4,40,2048]{3,2,1,0:T(8,128)(2,1)}), bf16[8,4,40,2048]{3,2,1,0:T(8,128)(2,1)}, u32[]{:S(2)}, u32[]{:S(2)}) async-start(bf16[8,4,40,2048]{3,2,1,0:T(8,128)(2,1)} %copy.173), calls=%async_computation.2 | async-start | bytes 10485760 | tf_op jit(solution)/shard_map/all_to_all | solution.py:57
  956.1 127.0 %all-gather.15.cloned.1.call-start = ((), (), s32[]{:S(2)}) async-start(), calls=%async_computation.26 | async-start | bytes 6553600 | tf_op jit(solution)/shard_map/all_gather | solution.py:53
  999.1 197.7 %reduce-scatter.22.cloned.1.call-start = ((), (), s32[]{:S(2)}) async-start(), calls=%async_computation.27 | async-start | bytes 6553600 | tf_op jit(solution)/shard_map/reduce_scatter | solution.py:307
  1068.9 119.9 %all-to-all-start.3 = ((bf16[8,4,40,2048]{3,2,1,0:T(8,128)(2,1)}), bf16[8,4,40,2048]{3,2,1,0:T(8,128)(2,1)}, u32[]{:S(2)}, u32[]{:S(2)}) async-start(bf16[8,4,40,2048]{3,2,1,0:T(8,128)(2,1)} %copy.185), calls=%async_computation.5 | async-start | bytes 10485760 | tf_op jit(solution)/shard_map/all_to_all | solution.py:57
  1188.8 119.6 %all-to-all-start.5 = ((bf16[8,4,40,2048]{3,2,1,0:T(8,128)(2,1)}), bf16[8,4,40,2048]{3,2,1,0:T(8,128)(2,1)}, u32[]{:S(2)}, u32[]{:S(2)}) async-start(bf16[8,4,40,2048]{3,2,1,0:T(8,128)(2,1)} %copy.188), calls=%async_computation.8 | async-start | bytes 10485760 | tf_op jit(solution)/shard_map/all_to_all | solution.py:57
  1308.3 119.6 %all-to-all-start.7 = ((bf16[8,4,40,2048]{3,2,1,0:T(8,128)(2,1)}), bf16[8,4,40,2048]{3,2,1,0:T(8,128)(2,1)}, u32[]{:S(2)}, u32[]{:S(2)}) async-start(bf16[8,4,40,2048]{3,2,1,0:T(8,128)(2,1)} %copy.196), calls=%async_computation.11 | async-start | bytes 10485760 | tf_op jit(solution)/shard_map/all_to_all | solution.py:57
  1316.3 216.7 %reduce-scatter.36.cloned.1.call-start = ((), (), s32[]{:S(2)}) async-start(), calls=%async_computation.35 | async-start | bytes 589824
  1470.9 127.0 %reduce-scatter.34.cloned.1.call-start = ((), (), s32[]{:S(2)}) async-start(), calls=%async_computation.34 | async-start | bytes 589824
  1498.8 163.6 %reduce-scatter.32.cloned.1.call-start = ((), (), s32[]{:S(2)}) async-start(), calls=%async_computation.33 | async-start | bytes 147456 | tf_op jit(solution)/shard_map/reduce_scatter | solution.py:442
  1502.9 198.8 %all-reduce.15.cloned.1.call-start = ((), (), s32[]{:S(2)}) async-start(), calls=%async_computation.36 | async-start | bytes 2097152 | tf_op jit(solution)/shard_map/psum | solution.py:405
  1603.2 163.0 %reduce-scatter.28.cloned.1.call-start = ((), (), s32[]{:S(2)}) async-start(), calls=%async_computation.31 | async-start | bytes 589824 | tf_op jit(solution)/shard_map/reduce_scatter | solution.py:433
  1606.5 224.2 %reduce-scatter.26.cloned.1.call-start = ((), (), s32[]{:S(2)}) async-start(), calls=%async_computation.30 | async-start | bytes 589824 | tf_op jit(solution)/shard_map/reduce_scatter | solution.py:430
  1609.7 312.3 %reduce-scatter.30.cloned.1.call-start = ((), (), s32[]{:S(2)}) async-start(), calls=%async_computation.32 | async-start | bytes 4718592 | tf_op jit(solution)/shard_map/reduce_scatter | solution.py:436
  1614.5 399.4 %reduce-scatter.24.cloned.1.call-start = ((), (), s32[]{:S(2)}) async-start(), calls=%async_computation.29 | async-start | bytes 4718592 | tf_op jit(solution)/shard_map/reduce_scatter | solution.py:427
  (150 other events, 4414.2 us)
Sparse Core Ops, SparseCore 0:
  10.2 85.8 all-gather.6
  98.2 81.2 all-gather.8
  288.4 37.7 all-reduce.16
  731.8 51.8 reduce-scatter.15
  849.5 52.8 reduce-scatter.17
  903.9 40.4 all-gather.10
  947.6 51.3 reduce-scatter.19
  1000.6 40.4 all-gather.12
  1042.7 40.4 all-gather.14
  1086.1 51.3 reduce-scatter.21
  1199.2 40.4 all-gather.16
  1471.0 61.9 reduce-scatter.35
  1536.9 60.9 reduce-scatter.33
  1602.0 60.3 reduce-scatter.31
  1665.4 36.2 all-reduce.14
  1704.8 61.2 reduce-scatter.27
  1769.7 60.9 reduce-scatter.25
  1834.2 87.8 reduce-scatter.29
  1926.1 87.6 reduce-scatter.23
where the time goes:
time: 2030 us; the launch traced here: 2020 us
  waiting for transfers between devices  1220 us (60%)
  blocking collectives  233 us (11%)
  local copies, waits for them, and re-layouts  188 us (9%)
  matrix products  185 us (9%)
  other arithmetic  107 us (5%)
  starting transfers between devices  71.2 us (4%)
    all_to_all x4, waiting for transfers between devices, carry_back(): lax.all_to_all(summed, 'fsdp', split_axis=0, concat_axis=0, tiled=True)  242 us
    all_to_all x2, waiting for transfers between devices, per_device(): lax.all_to_all(grad_outgoing, 'fsdp', split_axis=0, concat_axis=0, tiled=...  193 us
    all_to_all x2, waiting for transfers between devices, per_device(): lax.all_to_all(outgoing, 'fsdp', split_axis=0, concat_axis=0, tiled=True)  160 us
    all_gather x4, waiting for transfers between devices, widen(): return lax.all_gather(summed, 'tp', axis=3, tiled=True)  126 us
    reduce_scatter x1, waiting for transfers between devices, per_device(): lax.psum_scatter(acc_output.astype(jnp.bfloat16), 'fsdp', scatter_dimensi...  89.8 us
    reduce_scatter x1, waiting for transfers between devices, per_device(): lax.psum_scatter(acc_query.astype(jnp.bfloat16), 'fsdp', scatter_dimensio...  89.7 us
    unnamed x21, waiting for transfers between devices  88.6 us
    reduce_scatter x1, waiting for transfers between devices, per_device(): lax.psum_scatter(acc_key.astype(jnp.bfloat16), 'fsdp', scatter_dimension=...  63 us
  transfers between devices with their start and end apart: 27, of which 23 were waited for; matrix products, arithmetic and copies ran while one was open for 20% of the time, Pallas kernels for 0%

commit v1 on v0

--- a/solution.py
+++ b/solution.py
@@ -1,13 +1,520 @@
+import functools
 import math
 
 import jax
 import jax.numpy as jnp
 from jax import lax
+from jax.experimental import pallas as pl
+from jax.experimental.pallas import tpu as pltpu
 from jax.sharding import PartitionSpec as P
 
 norm_eps = 1e-06
 rope_base = 1000000.0
 masked_score = -1e30
+MESH = pl.DeviceIdType.MESH
+LOW = jnp.bfloat16
+F32 = jnp.float32
+VMEM_LIMIT = 60 * 2**20
+
+
+def coords():
+    f = lax.axis_index("fsdp")
+    t = lax.axis_index("tp")
+    return f // 2, f % 2, t // 2, t % 2
+
+
+def place(z, x, y, c):
+    return (2 * z + x, 2 * y + c)
+
+
+def greet(z, x, y, c):
+    barrier = pltpu.get_barrier_semaphore()
+    peers = [place(z, 1 - x, y, c), place(z, x, 1 - y, c), place(z, x, y, 1 - c)]
+    peers += [place((z + d) % 4, x, y, c) for d in (1, 2, 3)]
+    for peer in peers:
+        pl.semaphore_signal(barrier, inc=1, device_id=peer, device_id_type=MESH)
+    pl.semaphore_wait(barrier, len(peers))
+
+
+def push(src, dst, send_sem, recv_sem, device):
+    copy = pltpu.make_async_remote_copy(
+        src_ref=src, dst_ref=dst, send_sem=send_sem, recv_sem=recv_sem, device_id=device, device_id_type=MESH
+    )
+    copy.start()
+    return copy
+
+
+def landed(ref, sem, device):
+    pltpu.make_async_remote_copy(
+        src_ref=ref, dst_ref=ref, send_sem=sem, recv_sem=sem, device_id=device, device_id_type=MESH
+    ).wait_recv()
+
+
+def gather_kernel(whole, in_ref, out_ref, loc, sz, rz, sx, rx, sy, ry, sdx, rdx, sdy, rdy, sc, rc):
+    z, x, y, c = coords()
+    rows = in_ref.shape[1]
+    cols = in_ref.shape[2] // 4
+    half = rows // 2
+    f = 2 * z + x
+    t = 2 * y + c
+
+    def block(z_, x_, y_, c_, h=None):
+        first, count = ((2 * z_ + x_) * rows, rows) if h is None else ((2 * z_ + x_) * rows + h * half, half)
+        return out_ref.at[:, pl.ds(first, count), pl.ds((2 * y_ + c_) * cols, cols)]
+
+    def source(z_to, t_, first, count):
+        seqs = slice(None) if whole else pl.ds(z_to // 2, 1)
+        return in_ref.at[seqs, pl.ds(first, count), pl.ds(t_ * cols, cols)]
+
+    greet(z, x, y, c)
+    xn, yn, cn = place(z, 1 - x, y, c), place(z, x, 1 - y, c), place(z, x, y, 1 - c)
+    own_src = in_ref if whole else in_ref.at[pl.ds(z // 2, 1)]
+    own = pltpu.make_async_copy(own_src, out_ref.at[:, pl.ds(f * rows, rows), :], loc.at[0])
+    own.start()
+    order = (1, 3, 2)
+    sends = []
+    for d in order:
+        zd = (z + d) % 4
+        sends.append(push(source(zd, t, 0, rows), block(z, x, y, c), sz.at[d], rz.at[z], place(zd, x, y, c)))
+    sends.append(push(source(z, t, 0, rows), block(z, x, y, c), sx.at[z], rx.at[z], xn))
+    ty = 2 * (1 - y) + c
+    sends.append(push(source(z, ty, 0, half), block(z, x, 1 - y, c, 0), sdx.at[z], rdx.at[z], xn))
+    for d in order:
+        zd = (z + d) % 4
+        b = block(zd, x, y, c)
+        landed(b, rz.at[zd], xn)
+        sends.append(push(b, b, sx.at[zd], rx.at[zd], xn))
+        sends.append(push(b, b, sy.at[zd], ry.at[zd], yn))
+        sends.append(push(b, b, sc.at[0, zd], rc.at[0, zd], cn))
+    for d in (0,) + order:
+        zd = (z + d) % 4
+        b = block(zd, 1 - x, y, c)
+        landed(b, rx.at[zd], xn)
+        bh = block(zd, 1 - x, y, c, 1)
+        sends.append(push(bh, bh, sdy.at[zd], rdy.at[zd], yn))
+        sends.append(push(b, b, sc.at[1, zd], rc.at[1, zd], cn))
+        if d != 0:
+            b = block(zd, x, 1 - y, c)
+            landed(b, ry.at[zd], xn)
+            bh = block(zd, x, 1 - y, c, 0)
+            sends.append(push(bh, bh, sdx.at[zd], rdx.at[zd], xn))
+            sends.append(push(b, b, sc.at[2, zd], rc.at[2, zd], cn))
+    for d in (0,) + order:
+        zd = (z + d) % 4
+        landed(block(zd, 1 - x, 1 - y, c, 0), rdx.at[zd], xn)
+        landed(block(zd, 1 - x, 1 - y, c, 1), rdy.at[zd], xn)
+        b = block(zd, 1 - x, 1 - y, c)
+        sends.append(push(b, b, sc.at[3, zd], rc.at[3, zd], cn))
+    for d in (0,) + order:
+        zd = (z + d) % 4
+        if d != 0:
+            landed(block(zd, x, y, 1 - c), rc.at[0, zd], xn)
+            landed(block(zd, x, 1 - y, 1 - c), rc.at[2, zd], xn)
+        landed(block(zd, 1 - x, y, 1 - c), rc.at[1, zd], xn)
+        landed(block(zd, 1 - x, 1 - y, 1 - c), rc.at[3, zd], xn)
+    for copy in sends:
+        copy.wait_send()
+    own.wait()
+
+
+def gather_rows(value, whole):
+    count, rows, width = value.shape
+    dma = pltpu.SemaphoreType.DMA
+    return pl.pallas_call(
+        functools.partial(gather_kernel, whole),
+        out_shape=jax.ShapeDtypeStruct((count if whole else 1, rows * 8, width), value.dtype),
+        in_specs=[pl.BlockSpec(memory_space=pl.ANY)],
+        out_specs=pl.BlockSpec(memory_space=pl.ANY),
+        scratch_shapes=[dma((1,))] + [dma((4,))] * 10 + [dma((4, 4))] * 2,
+        compiler_params=pltpu.CompilerParams(collective_id=0 if whole else 1, has_side_effects=True),
+        name="gather_whole" if whole else "gather_half",
+    )(value)
+
+
+def add_into(target, *others):
+    count, rows, _ = target.shape
+    step = 32
+
+    @pl.loop(0, count * rows // step)
+    def _(i):
+        n = i // (rows // step)
+        r = pl.ds(pl.multiple_of((i % (rows // step)) * step, step), step)
+        total = target[n, r, :].astype(F32)
+        for other in others:
+            total = total + other[n, r, :].astype(F32)
+        target[n, r, :] = total.astype(target.dtype)
+
+
+def sum_kernel(whole, in_ref, out_ref, acc, fc, f1x, f1y, f2x, f2y, fz, full, tmp,
+               lsem, sc, rc, s1x, r1x, s1y, r1y, s2x, r2x, s2y, r2y, sz, rz, sg, rg, osem):
+    z, x, y, c = coords()
+    rows = out_ref.shape[1]
+    cols = out_ref.shape[2] // 4
+    half = rows // 2
+    xn, yn, cn = place(z, 1 - x, y, c), place(z, x, 1 - y, c), place(z, x, y, 1 - c)
+    lanes = ((x, y), (1 - x, y), (x, 1 - y), (1 - x, 1 - y))
+
+    def block(z_, lane, c_):
+        x_, y_ = lanes[lane]
+        return in_ref.at[:, pl.ds((2 * z_ + x_) * rows, rows), pl.ds((2 * y_ + c_) * cols, cols)]
+
+    greet(z, x, y, c)
+    sends = []
+    loads = {}
+    order = (2, 1, 3, 0)
+    for lane in (3, 1, 2, 0):
+        for d in order:
+            zd = (z + d) % 4
+            sends.append(push(block(zd, lane, 1 - c), fc.at[lane, d], sc.at[lane, d], rc.at[lane, d], cn))
+            loads[lane, d] = pltpu.make_async_copy(block(zd, lane, c), acc.at[lane, d], lsem.at[lane, d])
+            loads[lane, d].start()
+
+    def core_sum(lane, d):
+        loads[lane, d].wait()
+        landed(fc.at[lane, d], rc.at[lane, d], cn)
+        add_into(acc.at[lane, d], fc.at[lane, d])
+
+    top, low = pl.ds(0, half), pl.ds(half, half)
+    for d in order:
+        core_sum(3, d)
+        sends.append(push(acc.at[3, d, :, top], f1x.at[d], s1x.at[d], r1x.at[d], xn))
+        sends.append(push(acc.at[3, d, :, low], f1y.at[d], s1y.at[d], r1y.at[d], yn))
+    for d in order:
+        core_sum(1, d)
+        core_sum(2, d)
+        landed(f1y.at[d], r1y.at[d], yn)
+        add_into(acc.at[1, d, :, low], f1y.at[d])
+        sends.append(push(acc.at[1, d], f2x.at[d], s2x.at[d], r2x.at[d], xn))
+        landed(f1x.at[d], r1x.at[d], xn)
+        add_into(acc.at[2, d, :, top], f1x.at[d])
+        sends.append(push(acc.at[2, d], f2y.at[d], s2y.at[d], r2y.at[d], yn))
+    for d in order:
+        core_sum(0, d)
+        landed(f2x.at[d], r2x.at[d], xn)
+        landed(f2y.at[d], r2y.at[d], yn)
+        add_into(acc.at[0, d], f2x.at[d], f2y.at[d])
+        if d != 0:
+            zd = (z + d) % 4
+            sends.append(push(acc.at[0, d], fz.at[(4 - d) % 4], sz.at[d], rz.at[(4 - d) % 4], place(zd, x, y, c)))
+    t = 2 * y + c
+    for d in (1, 2, 3):
+        landed(fz.at[d], rz.at[d], cn)
+    step = 32
+
+    @pl.loop(0, 2 * rows // step)
+    def _(i):
+        n = i // (rows // step)
+        r = pl.ds(pl.multiple_of((i % (rows // step)) * step, step), step)
+        if whole:
+            total = acc[0, 0, n, r, :].astype(F32)
+            for d in (1, 2, 3):
+                total = total + fz[d, n, r, :].astype(F32)
+        else:
+            total = jnp.where(z // 2 == n, acc[0, 0, 0, r, :].astype(F32), 0.0)
+            for d in (1, 2, 3):
+                total = total + jnp.where(((z + d) % 4) // 2 == n, fz[d, 0, r, :].astype(F32), 0.0)
+        tmp[n, r, :] = total.astype(tmp.dtype)
+
+    mine = full.at[t]
+    keep = pltpu.make_async_copy(tmp, mine, osem.at[4])
+    keep.start()
+    sends.append(push(tmp, mine, sg.at[0], rg.at[0], yn))
+    sends.append(push(tmp, mine, sg.at[1], rg.at[1], cn))
+    ty, tc, td = 2 * (1 - y) + c, 2 * y + 1 - c, 2 * (1 - y) + 1 - c
+    landed(full.at[ty], rg.at[0], yn)
+    sends.append(push(full.at[ty], full.at[ty], sg.at[2], rg.at[2], cn))
+    landed(full.at[tc], rg.at[1], cn)
+    landed(full.at[td], rg.at[2], cn)
+    keep.wait()
+    outs = []
+    for q in range(4):
+        outs.append(pltpu.make_async_copy(full.at[q], out_ref.at[:, :, pl.ds(q * cols, cols)], osem.at[q]))
+        outs[-1].start()
+    for copy in sends:
+        copy.wait_send()
+    for copy in outs:
+        copy.wait()
+
+
+def sum_rows(value, whole):
+    count, total_rows, width = value.shape
+    rows, cols = total_rows // 8, width // 4
+    dma = pltpu.SemaphoreType.DMA
+    low = value.dtype
+    vm = pltpu.VMEM
+    return pl.pallas_call(
+        functools.partial(sum_kernel, whole),
+        out_shape=jax.ShapeDtypeStruct((2, rows, width), low),
+        in_specs=[pl.BlockSpec(memory_space=pl.ANY)],
+        out_specs=pl.BlockSpec(memory_space=pl.ANY),
+        scratch_shapes=[
+            vm((4, 4, count, rows, cols), low),
+            vm((4, 4, count, rows, cols), low),
+            vm((4, count, rows // 2, cols), low),
+            vm((4, count, rows // 2, cols), low),
+            vm((4, count, rows, cols), low),
+            vm((4, count, rows, cols), low),
+            vm((4, count, rows, cols), low),
+            vm((4, 2, rows, cols), low),
+            vm((2, rows, cols), low),
+            dma((4, 4)), dma((4, 4)), dma((4, 4)),
+        ] + [dma((4,))] * 10 + [dma((3,))] * 2 + [dma((5,))],
+        compiler_params=pltpu.CompilerParams(
+            collective_id=2 if whole else 3, has_side_effects=True, vmem_limit_bytes=VMEM_LIMIT
+        ),
+        name="sum_whole" if whole else "sum_half",
+    )(value)
+
+
+def dot_nn(a, b):
+    return jnp.dot(a, b, preferred_element_type=F32)
+
+
+def dot_nt(a, b):
+    return lax.dot_general(a, b, (((1,), (1,)), ((), ())), preferred_element_type=F32)
+
+
+def dot_tn(a, b):
+    return lax.dot_general(a, b, (((0,), (0,)), ((), ())), preferred_element_type=F32)
+
+
+def turn_half(values):
+    width = values.shape[-1]
+    lane = lax.broadcasted_iota(jnp.int32, values.shape, values.ndim - 1)
+    rolled = pltpu.roll(values, width // 2, values.ndim - 1)
+    return jnp.where(lane < width // 2, -rolled, rolled)
+
+
+def attend_kernel(heads, xn_ref, w_ref, cos_ref, sin_ref, qg_ref, kg_ref,
+                  pre_ref, qkv_ref, prob_ref, ctx_ref):
+    seq = xn_ref.shape[0]
+    hd = cos_ref.shape[1]
+    tile = 256
+    scale = 1.0 / math.sqrt(hd)
+    for i in range(seq // tile):
+        r = pl.ds(i * tile, tile)
+        pre = dot_nn(xn_ref[r, :], w_ref[...])
+        pre_ref[r, :] = pre[:, : (heads + 1) * hd]
+        qkv_ref[r, pl.ds((heads + 1) * hd, hd)] = pre[:, (heads + 1) * hd :].astype(LOW)
+        for a in range(heads + 1):
+            one = pre[:, a * hd : (a + 1) * hd]
+            factor = lax.rsqrt(jnp.mean(one * one, axis=-1, keepdims=True) + norm_eps)
+            gained = one * factor * (qg_ref if a < heads else kg_ref)[...]
+            turned = gained * cos_ref[r, :] + turn_half(gained) * sin_ref[r, :]
+            qkv_ref[r, pl.ds(a * hd, hd)] = turned.astype(LOW)
+    for a in range(heads):
+        for i in range(seq // tile):
+            r = pl.ds(i * tile, tile)
+            n = (i + 1) * tile
+            query = qkv_ref[r, pl.ds(a * hd, hd)]
+            key = qkv_ref[pl.ds(0, n), pl.ds(heads * hd, hd)]
+            value = qkv_ref[pl.ds(0, n), pl.ds((heads + 1) * hd, hd)]
+            score = dot_nt(query, key) * scale
+            row = lax.broadcasted_iota(jnp.int32, (tile, n), 0) + i * tile
+            col = lax.broadcasted_iota(jnp.int32, (tile, n), 1)
+            score = jnp.where(col <= row, score, masked_score)
+            peak = jnp.max(score, axis=-1, keepdims=True)
+            terms = jnp.exp(score - peak)
+            prob = (terms * (1.0 / jnp.sum(terms, axis=-1, keepdims=True))).astype(LOW)
+            prob_ref[a, r, pl.ds(0, n)] = prob
+            ctx_ref[r, pl.ds(a * hd, hd)] = dot_nn(prob, value).astype(LOW)
+
+
+def attend(xn, weights, cosine, sine, query_gain, key_gain):
+    seq = xn.shape[0]
+    hd = query_gain.shape[0]
+    heads = weights.shape[1] // hd - 2
+    return pl.pallas_call(
+        functools.partial(attend_kernel, heads),
+        out_shape=(
+            jax.ShapeDtypeStruct((seq, (heads + 1) * hd), F32),
+            jax.ShapeDtypeStruct((seq, (heads + 2) * hd), LOW),
+            jax.ShapeDtypeStruct((heads, seq, seq), LOW),
+            jax.ShapeDtypeStruct((seq, heads * hd), LOW),
+        ),
+        compiler_params=pltpu.CompilerParams(vmem_limit_bytes=VMEM_LIMIT),
+        name="attend",
+    )(xn, weights, cosine, sine, query_gain[None], key_gain[None])
+
+
+def attend_back_kernel(heads, dctx_ref, pre_ref, qkv_ref, prob_ref, cos_ref, sin_ref, qg_ref, kg_ref,
+                       dqkv_ref, gains_ref, dq_s, dk_s, dv_s):
+    seq = dctx_ref.shape[0]
+    hd = cos_ref.shape[1]
+    tile = 256
+    scale = 1.0 / math.sqrt(hd)
+    dk_s[...] = jnp.zeros_like(dk_s)
+    dv_s[...] = jnp.zeros_like(dv_s)
+    for a in range(heads):
+        for i in range(seq // tile):
+            r = pl.ds(i * tile, tile)
+            n = (i + 1) * tile
+            query = qkv_ref[r, pl.ds(a * hd, hd)]
+            key = qkv_ref[pl.ds(0, n), pl.ds(heads * hd, hd)]
+            value = qkv_ref[pl.ds(0, n), pl.ds((heads + 1) * hd, hd)]
+            dctx = dctx_ref[r, pl.ds(a * hd, hd)]
+            prob = prob_ref[a, r, pl.ds(0, n)]
+            wide = prob.astype(F32)
+            dprob = dot_nt(dctx, value)
+            delta = jnp.sum(wide * dprob, axis=-1, keepdims=True)
+            dscore = (wide * (dprob - delta)).astype(LOW)
+            dq_s[r, pl.ds(a * hd, hd)] = dot_nn(dscore, key) * scale
+            dk_s[pl.ds(0, n), :] += dot_tn(dscore, query) * scale
+            dv_s[pl.ds(0, n), :] += dot_tn(prob, dctx)
+    gq = jnp.zeros((1, hd), F32)
+    gk = jnp.zeros((1, hd), F32)
+    for i in range(seq // tile):
+        r = pl.ds(i * tile, tile)
+        dqkv_ref[r, pl.ds((heads + 1) * hd, hd)] = dv_s[r, :].astype(LOW)
+        for a in range(heads + 1):
+            up = dq_s[r, pl.ds(a * hd, hd)] if a < heads else dk_s[r, :]
+            one = pre_ref[r, pl.ds(a * hd, hd)]
+            factor = lax.rsqrt(jnp.mean(one * one, axis=-1, keepdims=True) + norm_eps)
+            hat = one * factor
+            turned = up * cos_ref[r, :] - turn_half(up * sin_ref[r, :])
+            part = jnp.sum(turned * hat, axis=0, keepdims=True)
+            gained = turned * (qg_ref if a < heads else kg_ref)[...]
+            back = factor * (gained - hat * jnp.mean(gained * hat, axis=-1, keepdims=True))
+            dqkv_ref[r, pl.ds(a * hd, hd)] = back.astype(LOW)
+            if a < heads:
+                gq = gq + part
+            else:
+                gk = gk + part
+    gains_ref[...] = jnp.concatenate([gq, gk], axis=0)
+
+
+def attend_back(dctx, pre, qkv, prob, cosine, sine, query_gain, key_gain):
+    seq = dctx.shape[0]
+    hd = query_gain.shape[0]
+    heads = prob.shape[0]
+    return pl.pallas_call(
+        functools.partial(attend_back_kernel, heads),
+        out_shape=(
+            jax.ShapeDtypeStruct((seq, (heads + 2) * hd), LOW),
+            jax.ShapeDtypeStruct((2, hd), F32),
+        ),
+        scratch_shapes=[
+            pltpu.VMEM((seq, heads * hd), F32),
+            pltpu.VMEM((seq, hd), F32),
+            pltpu.VMEM((seq, hd), F32),
+        ],
+        compiler_params=pltpu.CompilerParams(vmem_limit_bytes=VMEM_LIMIT),
+        name="attend_back",
+    )(dctx, pre, qkv, prob, cosine, sine, query_gain[None], key_gain[None])
+
+
+def route_probs(logits, ids, count):
+    lane = lax.broadcasted_iota(jnp.int32, logits.shape, 1)
+    named = lane == ids[:, 0:1]
+    for k in range(1, count):
+        named = named | (lane == ids[:, k : k + 1])
+    masked = jnp.where(named, logits, masked_score)
+    terms = jnp.where(named, jnp.exp(masked - jnp.max(masked, axis=-1, keepdims=True)), 0.0)
+    return terms / jnp.sum(terms, axis=-1, keepdims=True)
+
+
+def experts_kernel(experts, route_count, first_ref, x_ref, og_ref, ids_ref, router_ref, g_ref, u_ref, d_ref,
+                   out_ref, dx_ref, dgp_ref, dg_ref, du_ref, dd_ref, dg_s, du_s, dd_s, sem):
+    i = pl.program_id(0)
+    hidden = g_ref.shape[0]
+    per = hidden // experts
+    tile = x_ref.shape[0]
+
+    @pl.when(i == 0)
+    def _():
+        dg_s[...] = jnp.zeros_like(dg_s)
+        du_s[...] = jnp.zeros_like(du_s)
+        dd_s[...] = jnp.zeros_like(dd_s)
+
+    x = x_ref[...]
+    og = og_ref[...]
+    first = first_ref[0]
+    probs = route_probs(dot_nn(x, router_ref[...]), ids_ref[...], route_count)
+    lanes = probs.shape[1]
+    row = lax.broadcasted_iota(jnp.int32, (lanes, hidden), 0)
+    col = lax.broadcasted_iota(jnp.int32, (lanes, hidden), 1)
+    spread = jnp.where(row == first + col // per, 1.0, 0.0).astype(LOW)
+    high = probs.astype(LOW)
+    rest = (probs - high.astype(F32)).astype(LOW)
+    share = dot_nn(high, spread) + dot_nn(rest, spread)
+    gate = dot_nt(x, g_ref[...])
+    up = dot_nt(x, u_ref[...])
+    raw = dot_nt(og, d_ref[...])
+    sig = 1.0 / (1.0 + jnp.exp(-gate))
+    act = gate * sig
+    inner = act * up
+    weighted = (inner * share).astype(LOW)
+    product = jnp.where(share > 0.0, inner * raw, 0.0)
+    product_high = product.astype(LOW)
+    product_rest = (product - product_high.astype(F32)).astype(LOW)
+    dgp_ref[...] = dot_nt(product_high, spread) + dot_nt(product_rest, spread)
+    d_inner = raw * share
+    d_up = (d_inner * act).astype(LOW)
+    d_gate = (d_inner * up * sig * (1.0 + gate * (1.0 - sig))).astype(LOW)
+    dx_ref[...] = (dot_nn(d_gate, g_ref[...]) + dot_nn(d_up, u_ref[...])).astype(LOW)
+    out_ref[...] = dot_nn(weighted, d_ref[...]).astype(LOW)
+    dg_s[...] += dot_tn(d_gate, x)
+    du_s[...] += dot_tn(d_up, x)
+    dd_s[...] += dot_tn(weighted, og)
+
+    @pl.when(i == pl.num_programs(0) - 1)
+    def _():
+        copies = []
+        for n, (src, dst) in enumerate(((dg_s, dg_ref), (du_s, du_ref), (dd_s, dd_ref))):
+            copies.append(pltpu.make_async_copy(src, dst, sem.at[n]))
+            copies[-1].start()
+        for copy in copies:
+            copy.wait()
+
+
+def run_experts(first, x, og, ids, router, gate, up, down):
+    tokens, width = x.shape
+    experts, per, _ = gate.shape
+    hidden = experts * per
+    tile = 256
+    lanes = router.shape[1]
+    once = pl.Buffered(1)
+    keep = lambda i, s: (0, 0)
+    walk = lambda i, s: (i, 0)
+    any_space = pl.BlockSpec(memory_space=pl.ANY)
+    grads = jax.ShapeDtypeStruct((hidden, width), F32)
+    return pl.pallas_call(
+        functools.partial(experts_kernel, experts, ids.shape[1]),
+        grid_spec=pltpu.PrefetchScalarGridSpec(
+            num_scalar_prefetch=1,
+            grid=(tokens // tile,),
+            in_specs=[
+                pl.BlockSpec((tile, width), walk),
+                pl.BlockSpec((tile, width), walk),
+                pl.BlockSpec((tile, ids.shape[1]), walk),
+                pl.BlockSpec((width, lanes), keep, pipeline_mode=once),
+                pl.BlockSpec((hidden, width), keep, pipeline_mode=once),
+                pl.BlockSpec((hidden, width), keep, pipeline_mode=once),
+                pl.BlockSpec((hidden, width), keep, pipeline_mode=once),
+            ],
+            out_specs=[
+                pl.BlockSpec((tile, width), walk),
+                pl.BlockSpec((tile, width), walk),
+                pl.BlockSpec((tile, lanes), walk),
+                any_space,
+                any_space,
+                any_space,
+            ],
+            scratch_shapes=[pltpu.VMEM((hidden, width), F32)] * 3 + [pltpu.SemaphoreType.DMA((3,))],
+        ),
+        out_shape=(
+            jax.ShapeDtypeStruct((tokens, width), LOW),
+            jax.ShapeDtypeStruct((tokens, width), LOW),
+            jax.ShapeDtypeStruct((tokens, lanes), F32),
+            grads,
+            grads,
+            grads,
+        ),
+        compiler_params=pltpu.CompilerParams(
+            vmem_limit_bytes=VMEM_LIMIT, dimension_semantics=("arbitrary",)
+        ),
+        name="experts",
+    )(first, x, og, ids, router, gate.reshape(hidden, width), up.reshape(hidden, width), down.reshape(hidden, width))
 
 
 def rotate_half(values):
@@ -62,7 +569,7 @@
     return arrived_home
 
 
-def per_device(
+def general_device(
     tokens,
     cotangent,
     expert_ids,
@@ -461,9 +968,154 @@
     )
 
 
+def small_device(
+    tokens,
+    cotangent,
+    expert_ids,
+    attention_gain,
+    query_gain,
+    key_gain,
+    query_weight,
+    key_weight,
+    value_weight,
+    output_weight,
+    expert_gain,
+    router_weight,
+    gate_weight,
+    up_weight,
+    down_weight,
+):
+    count, rows, width = tokens.shape
+    hd = query_gain.shape[0]
+    f = lax.axis_index("fsdp")
+    n_fsdp = lax.axis_size("fsdp")
+    seq = rows * n_fsdp
+    experts = gate_weight.shape[0]
+    expert_count = experts * n_fsdp
+    local = query_weight.shape[1]
+    pairs = n_fsdp // count
+    part = local // pairs
+    piece = query_weight.shape[0]
+
+    cosine, sine = rope_tables(jnp.arange(seq, dtype=jnp.int32), hd)
+    inputs = tokens.astype(F32)
+    input_hat, attention_factor = norm_parts(inputs)
+    normed = (input_hat * attention_gain).astype(LOW)
+
+    def fetch(weight):
+        cut = weight.reshape(piece, pairs, part).transpose(1, 0, 2)
+        cut = jnp.concatenate([cut] * count, axis=0)
+        return lax.all_to_all(cut, "fsdp", split_axis=0, concat_axis=0, tiled=True).reshape(width, part)
+
+    def give_back(grad):
+        cut = lax.all_to_all(
+            grad.astype(LOW).reshape(n_fsdp, piece, part), "fsdp", split_axis=0, concat_axis=0, tiled=True
+        ).astype(F32)
+        cut = jnp.sum(cut.reshape(count, pairs, piece, part), axis=0)
+        return cut.transpose(1, 0, 2).reshape(piece, local)
+
+    query_pair = fetch(query_weight)
+    output_pair = fetch(output_weight)
+    key_value = lax.all_gather(
+        jnp.concatenate([key_weight, value_weight], axis=1), "fsdp", axis=0, tiled=True
+    )
+    router_full = lax.all_gather(router_weight, "fsdp", axis=0, tiled=True)
+    ids_all = lax.all_gather(expert_ids, "fsdp", axis=1, tiled=True)
+
+    normed_all = gather_rows(normed, False)[0]
+    weights = jnp.concatenate([query_pair, key_value], axis=1)
+    pre, qkv, prob, context = attend(normed_all, weights, cosine, sine, query_gain, key_gain)
+    branch_part = lax.dot_general(
+        context, output_pair, (((1,), (1,)), ((), ())), preferred_element_type=F32
+    ).astype(LOW)
+    branch = sum_rows(branch_part[None], False)
+    resid = inputs + branch.astype(F32)
+    resid_hat, expert_factor = norm_parts(resid)
+    expert_in = (resid_hat * expert_gain).astype(LOW)
+
+    expert_all = gather_rows(expert_in, True).reshape(count * seq, width)
+    grad_all = gather_rows(cotangent, True).reshape(count * seq, width)
+    lanes = 128
+    router_wide = jnp.pad(router_full, ((0, 0), (0, lanes - expert_count)))
+    first = (f * experts).astype(jnp.int32).reshape(1)
+    out_part, dx_part, dgp_part, d_gate, d_up, d_down = run_experts(
+        first,
+        expert_all,
+        grad_all,
+        ids_all.reshape(count * seq, -1),
+        router_wide,
+        gate_weight,
+        up_weight,
+        down_weight,
+    )
+    dgp_part = dgp_part[:, :expert_count].reshape(count, seq, expert_count)
+    d_gate_probs = lax.psum(
+        lax.psum_scatter(dgp_part, "fsdp", scatter_dimension=1, tiled=True), "tp"
+    )
+    dx_sum = sum_rows(dx_part.reshape(count, seq, width), True).astype(F32)
+    out_sum = sum_rows(out_part.reshape(count, seq, width), True).astype(F32)
+    layer_output = (resid + out_sum).astype(LOW)
+
+    expert_range = jnp.arange(expert_count, dtype=jnp.int32)
+    named = jnp.any(expert_ids[..., None] == expert_range, axis=2)
+    logits = jnp.dot(expert_in, router_full, preferred_element_type=F32)
+    masked = jnp.where(named, logits, masked_score)
+    terms = jnp.where(named, jnp.exp(masked - jnp.max(masked, axis=-1, keepdims=True)), 0.0)
+    gate_probs = terms / jnp.sum(terms, axis=-1, keepdims=True)
+    d_logits = (
+        gate_probs * (d_gate_probs - jnp.sum(gate_probs * d_gate_probs, axis=-1, keepdims=True))
+    ).astype(LOW)
+    d_expert_in = dx_sum + lax.dot_general(
+        d_logits, router_full, (((2,), (1,)), ((), ())), preferred_element_type=F32
+    )
+    router_part = lax.dot_general(
+        expert_in, d_logits, (((0, 1), (0, 1)), ((), ())), preferred_element_type=F32
+    )
+    expert_gain_part = jnp.sum(d_expert_in * resid_hat, axis=(0, 1))
+    out_grad = cotangent.astype(F32)
+    d_resid = out_grad + norm_back(d_expert_in, expert_gain, resid_hat, expert_factor)
+    d_branch = d_resid.astype(LOW)
+
+    branch_all = gather_rows(d_branch, False)[0]
+    d_context = jnp.dot(branch_all, output_pair, preferred_element_type=F32).astype(LOW)
+    d_output = lax.dot_general(branch_all, context, (((0,), (0,)), ((), ())), preferred_element_type=F32)
+    d_qkv, head_gains = attend_back(d_context, pre, qkv, prob, cosine, sine, query_gain, key_gain)
+    d_normed_part = lax.dot_general(
+        d_qkv, weights, (((1,), (1,)), ((), ())), preferred_element_type=F32
+    ).astype(LOW)
+    d_weights = lax.dot_general(normed_all, d_qkv, (((0,), (0,)), ((), ())), preferred_element_type=F32)
+    d_normed = sum_rows(d_normed_part[None], False).astype(F32)
+    attention_gain_part = jnp.sum(d_normed * input_hat, axis=(0, 1))
+    input_grad = (d_resid + norm_back(d_normed, attention_gain, input_hat, attention_factor)).astype(LOW)
+
+    head_gains = lax.psum(head_gains, "tp")
+
+    def scattered(value):
+        return lax.psum_scatter(value, "fsdp", scatter_dimension=0, tiled=True)
+
+    d_key_value = scattered(d_weights[:, part:].astype(LOW)).astype(F32)
+    return (
+        layer_output,
+        input_grad,
+        scattered(attention_gain_part),
+        scattered(head_gains[0]),
+        scattered(head_gains[1]),
+        give_back(d_weights[:, :part]),
+        d_key_value[:, :hd],
+        d_key_value[:, hd:],
+        give_back(d_output),
+        scattered(expert_gain_part),
+        scattered(router_part),
+        d_gate.reshape(gate_weight.shape),
+        d_up.reshape(up_weight.shape),
+        d_down.reshape(down_weight.shape),
+    )
+
+
 def solution(mesh):
+    body = small_device if (mesh.shape["fsdp"], mesh.shape["tp"]) == (8, 4) else general_device
     return jax.shard_map(
-        per_device,
+        body,
         mesh=mesh,
         in_specs=(
             P(None, "fsdp", None),

time: 2030 us -> 802 us (0.40)
  waiting for transfers between devices: 1220 us -> 85.7 us
  Pallas kernels: 0 us -> 492 us
  local copies, waits for them, and re-layouts: 188 us -> 17.2 us
  matrix products: 185 us -> 27.6 us
  blocking collectives: 233 us -> 106 us
  other arithmetic: 107 us -> 26 us
  starting transfers between devices: 71.2 us -> 25 us
    all_to_all x8 -> x4, waiting for transfers between devices: 595 us -> 24.6 us  [the longest x2 24.6 us: fetch(): lax.all_to_all(cut, 'fsdp', split_axis=0, concat_axis=0, tiled=True)]
    pallas_call x0 -> x11, Pallas kernels: none -> 492 us  [the longest x4 199 us: sum_rows(): pl.pallas_call(functools.partial(sum_kernel, whole), out_shape=jax.ShapeD...]
    reduce_scatter x9 -> x3, waiting for transfers between devices: 372 us -> 61.1 us  [the longest x2 49.9 us: scattered(): return lax.psum_scatter(value, 'fsdp', scatter_dimension=0, tiled=True)]
    dot_general x76 -> x7, matrix products: 185 us -> 26.1 us  [the longest x1 6.16 us: small_device(): lax.dot_general(d_qkv, weights, (((1,), (1,)), ((), ())), preferred_eleme...]
    all_gather x7 -> x2, blocking collectives: 210 us -> 58.3 us  [the longest x1 31.5 us: small_device(): router_full = lax.all_gather(router_weight, 'fsdp', axis=0, tiled=True)]
    all_gather x6 -> x1, waiting for transfers between devices: 126 us -> 0.01 us  [small_device(): lax.all_gather(jnp.concatenate([key_weight, value_weight], axis=1), 'fsdp...]
    gather x8 -> x0, local copies, waits for them, and re-layouts: 99.5 us -> none  [the longest x2 27.1 us: per_device(): jnp.concatenate([d_route, zero_row], axis=0)[slot_source]]
    unnamed x21 -> x4, waiting for transfers between devices: 88.6 us -> 0.07 us
  transfers between devices with their start and end apart: 27 -> 8, of which waited for: 23 -> 3; matrix products, arithmetic and copies ran while one was open for 20% -> 6% of each run, Pallas kernels for 0% -> 36%
where the time goes in v1:
time: 802 us; the launch traced here: 795 us
  Pallas kernels  492 us (61%)
  blocking collectives  106 us (13%)
  waiting for transfers between devices  85.7 us (11%)
  matrix products  27.6 us (3%)
  other arithmetic  26 us (3%)
  starting transfers between devices  25 us (3%)
  local copies, waits for them, and re-layouts  17.2 us (2%)
  between operations  15.7 us (2%)
    pallas_call x4, Pallas kernels, sum_rows(): pl.pallas_call(functools.partial(sum_kernel, whole), out_shape=jax.ShapeD...  199 us
    pallas_call x4, Pallas kernels, gather_rows(): pl.pallas_call(functools.partial(gather_kernel, whole), out_shape=jax.Sha...  182 us
    pallas_call x1, Pallas kernels, run_experts(): pl.pallas_call(functools.partial(experts_kernel, experts, ids.shape[1]),...  86.7 us
    reduce_scatter x2, waiting for transfers between devices, scattered(): return lax.psum_scatter(value, 'fsdp', scatter_dimension=0, tiled=True)  49.9 us
    all_gather x1, blocking collectives, small_device(): router_full = lax.all_gather(router_weight, 'fsdp', axis=0, tiled=True)  31.5 us
    unnamed x1, blocking collectives  29.5 us
    all_gather x1, blocking collectives, small_device(): ids_all = lax.all_gather(expert_ids, 'fsdp', axis=1, tiled=True)  26.9 us
    all_to_all x2, waiting for transfers between devices, fetch(): lax.all_to_all(cut, 'fsdp', split_axis=0, concat_axis=0, tiled=True)  24.6 us
  transfers between devices with their start and end apart: 8, of which 3 were waited for; matrix products, arithmetic and copies ran while one was open for 6% of the time, Pallas kernels for 36%

profile of v1, /device:TPU:16, one launch (start us, length us, event | category | flops | bytes accessed | tf_op | source)
XLA Modules:
  0.0 795.4 jit_solution(11237185244158579347)
XLA Ops:
  9.4 6.1 all-to-all-start
  17.5 24.5 %all-to-all-done = bf16[8,256,256]{2,1,0:T(8,128)(2,1)S(1)} async-done(((bf16[8,256,256]{2,1,0:T(8,128)(2,1)}), bf16[8,256,256]{2,1,0:T(8,128)(2,1)S(1)}, u32[]{:S(2)}, u32[]{:S(2)}) %all-to-all-start) | async-done | bytes 1048608 | tf_op jit(solution)/shard_map/all_to_all | solution.py:1008
  42.1 6.9 all-to-all-start.1
  50.6 54.6 %gather_half.2 = bf16[1,1024,2048]{2,1,0:T(8,128)(2,1)} custom-call(bf16[2,128,2048]{2,1,0:T(8,128)(2,1)} %fusion.16.in_ref), custom_call_target="tpu_custom_call" | custom-call | tf_op jit(solution)/shard_map/gather_half/pallas_call | solution.py:123
  105.3 50.2 %gather_whole.3 = bf16[2,1024,2048]{2,1,0:T(8,128)(2,1)} custom-call(bf16[2,128,2048]{2,1,0:T(8,128)(2,1)} %in_ref.1), custom_call_target="tpu_custom_call" | custom-call | tf_op jit(solution)/shard_map/gather_whole/pallas_call | solution.py:123
  155.6 26.9 %all_gather.10 = s32[2,1024,8]{1,2,0:T(8,128)S(1)} all-gather(s32[2,128,8]{1,2,0:T(8,128)S(1)} %copy-done.15), channel_id=1, replica_groups=mesh['fsdp'=8,'tp'=4] {'fsdp'}, dimensions={1}, use_global_device_ids=true | all-gather | bytes 73728 | tf_op jit(solution)/shard_map/all_gather | solution.py:1023
  183.8 31.5 %all_gather.11 = bf16[2048,32]{1,0:T(8,128)(2,1)S(1)} all-gather(bf16[256,32]{1,0:T(8,128)(2,1)S(1)} %copy.78), channel_id=1, replica_groups=mesh['fsdp'=8,'tp'=4] {'fsdp'}, dimensions={0}, use_global_device_ids=true | all-gather | bytes 147456 | tf_op jit(solution)/shard_map/all_gather | solution.py:1022
  222.4 11.8 %attend.1 = (f32[1024,384]{1,0:T(8,128)}, bf16[1024,512]{1,0:T(8,128)(2,1)}, bf16[2,1024,1024]{2,1,0:T(8,128)(2,1)}, bf16[1024,256]{1,0:T(8,128)(2,1)}) custom-call(bf16[1024,2048]{1,0:T(8,128)(2,1)} %bitcast.83, bf16[2048,512]{1,0:T(8,128)(2,1)} %pad_maximum_fusion.w_ref, f32[1024,128]{1,0:T(8,128)} %get-tuple-element.79.cos_ref, ...), custom_call_target="tpu_custom_call" | custom-call | tf_op jit(solution)/shard_map/attend/pallas_call | solution.py:327
  239.5 40.6 %sum_half.2 = bf16[2,128,2048]{2,1,0:T(8,128)(2,1)} custom-call(bf16[1,1024,2048]{2,1,0:T(8,128)(2,1)} %convert_bitcast_fusion.1.in_ref), custom_call_target="tpu_custom_call" | custom-call | tf_op jit(solution)/shard_map/sum_half/pallas_call | solution.py:245
  283.3 49.5 %gather_whole.2 = bf16[2,1024,2048]{2,1,0:T(8,128)(2,1)} custom-call(bf16[2,128,2048]{2,1,0:T(8,128)(2,1)} %multiply_convert_fusion.in_ref), custom_call_target="tpu_custom_call" | custom-call | tf_op jit(solution)/shard_map/gather_whole/pallas_call | solution.py:123
  332.9 86.7 %experts.1 = (bf16[2048,2048]{1,0:T(8,128)(2,1)}, bf16[2048,2048]{1,0:T(8,128)(2,1)}, f32[2048,128]{1,0:T(8,128)}, f32[768,2048]{1,0:T(8,128)}, f32[768,2048]{1,0:T(8,128)}, /*index=5*/f32[768,2048]{1,0:T(8,128)}) custom-call(s32[1]{0:T(128)} %bitcast.9.first_ref, bf16[2048,2048]{1,0:T(8,128)(2,1)} %bitcast.82, bf16[2048,2048]{1,0:T(8,128)(2,1)} %bitcast.81, ...), custom_call_target="tpu_custom_call" | custom-call | tf_op jit(solution)/shard_map/experts/pallas_call | solution.py:481
  422.0 56.3 %sum_whole.3 = bf16[2,128,2048]{2,1,0:T(8,128)(2,1)} custom-call(bf16[2,1024,2048]{2,1,0:T(8,128)(2,1)} %bitcast.85), custom_call_target="tpu_custom_call" | custom-call | tf_op jit(solution)/shard_map/sum_whole/pallas_call | solution.py:245
  479.7 11.2 %reduce-scatter.4.cloned.1.call-done = f32[2,128,32]{1,2,0:T(8,128)} async-done(((f32[2,1024,32]{1,2,0:T(8,128)}), f32[2,128,32]{1,2,0:T(8,128)}) %reduce-scatter.4.cloned.1.call-update) | async-done | bytes 32784 | tf_op jit(solution)/shard_map/reduce_scatter | solution.py:1053
  490.9 11.0 %psum.14 = f32[2,128,32]{1,2,0:T(8,128)S(1)} all-reduce(f32[2,128,32]{1,2,0:T(8,128)} %reduce-scatter.4.cloned.1.call-done), channel_id=1, replica_groups=mesh['fsdp'=8,'tp'=4] {'tp'}, use_global_device_ids=true, to_apply=%region_6.7 | all-reduce | flops 8192 | bytes 65536 | tf_op jit(solution)/shard_map/psum | solution.py:1052
  507.7 27.8 %gather_half.3 = bf16[1,1024,2048]{2,1,0:T(8,128)(2,1)} custom-call(bf16[2,128,2048]{2,1,0:T(8,128)(2,1)} %fusion.32.in_ref), custom_call_target="tpu_custom_call" | custom-call | tf_op jit(solution)/shard_map/gather_half/pallas_call | solution.py:123
  542.3 5.6 all-to-all-start.3
  547.9 12.0 %attend_back.1 = (bf16[1024,512]{1,0:T(8,128)(2,1)}, f32[2,128]{1,0:T(2,128)}) custom-call(bf16[1024,256]{1,0:T(8,128)(2,1)} %fusion.21.dctx_ref, f32[1024,384]{1,0:T(8,128)} %get-tuple-element.30.pre_ref, bf16[1024,512]{1,0:T(8,128)(2,1)} %get-tuple-element.31.qkv_ref, bf16[2,1024,1024]{2,1,0:T(8,128)(2,1)} %get-tuple-element.32.prob_ref, ...), custom_call_target="tpu_custom_call" | custom-call | tf_op jit(solution)/shard_map/attend_back/pallas_call | solution.py:390
  568.2 60.3 %sum_whole.2 = bf16[2,128,2048]{2,1,0:T(8,128)(2,1)} custom-call(bf16[2,1024,2048]{2,1,0:T(8,128)(2,1)} %bitcast.84), custom_call_target="tpu_custom_call" | custom-call | tf_op jit(solution)/shard_map/sum_whole/pallas_call | solution.py:245
  628.5 6.2 all-to-all-start.2
  634.9 6.2 convert_bitcast_fusion.in_ref
  641.1 42.3 %sum_half.3 = bf16[2,128,2048]{2,1,0:T(8,128)(2,1)} custom-call(bf16[1,1024,2048]{2,1,0:T(8,128)(2,1)} %convert_bitcast_fusion.in_ref), custom_call_target="tpu_custom_call" | custom-call | tf_op jit(solution)/shard_map/sum_half/pallas_call | solution.py:245
  683.4 7.2 psum.15
  692.5 29.5 %all-reduce.5 = (f32[2048]{0:T(1024)S(1)}, f32[128]{0:T(128)S(1)}, f32[128]{0:T(128)S(1)}, f32[2048]{0:T(1024)S(1)}) all-reduce(f32[2048]{0:T(1024)S(1)} %get-tuple-element.68, f32[128]{0:T(128)S(1)} %get-tuple-element.83, f32[128]{0:T(128)S(1)} %get-tuple-element.82, ...), channel_id=3, replica_groups=mesh['fsdp'=8,'tp'=4] {'fsdp'}, use_global_device_ids=true, to_apply=%region_11.12.clone | all-reduce | flops 4352 | bytes 34816
  738.7 49.9 %reduce-scatter.8.cloned.1.call-done = f32[256,32]{0,1:T(8,128)} async-done(((f32[2048,32]{0,1:T(8,128)}), f32[256,32]{0,1:T(8,128)}) %reduce-scatter.8.cloned.1.call-update) | async-done | bytes 32784 | tf_op jit(solution)/shard_map/reduce_scatter | solution.py:1094
  (101 shorter events, 65.0 us)
Async XLA Ops:
  8.3 7.2 copy-start.13
  8.3 7.2 copy-start.14
  8.3 7.9 copy-start.10
  9.4 32.7 %all-to-all-start = ((bf16[8,256,256]{2,1,0:T(8,128)(2,1)}), bf16[8,256,256]{2,1,0:T(8,128)(2,1)S(1)}, u32[]{:S(2)}, u32[]{:S(2)}) async-start(bf16[8,256,256]{2,1,0:T(8,128)(2,1)} %pad_maximum_fusion.1), calls=%async_computation | async-start | bytes 2097152 | tf_op jit(solution)/shard_map/all_to_all | solution.py:1008
  15.5 203.9 %all-gather.2.cloned.1.call-start = ((), (), s32[]{:S(2)}) async-start(), calls=%async_computation.7 | async-start | bytes 1179648 | tf_op jit(solution)/shard_map/all_gather | solution.py:1019
  16.4 32.5 %copy-start = (bf16[2,128,2048]{2,1,0:T(8,128)(2,1)S(1)}, bf16[2,128,2048]{2,1,0:T(8,128)(2,1)}, u32[]{:S(2)}) copy-start(bf16[2,128,2048]{2,1,0:T(8,128)(2,1)} %param.15) | copy-start | bytes 3145732
  16.4 32.8 %copy-start.12 = (f32[2048]{0:T(1024)S(1)}, f32[2048]{0:T(1024)}, u32[]{:S(2)}) copy-start(f32[2048]{0:T(1024)} %param.18) | copy-start | bytes 24580
  42.1 8.5 %copy-start.7 = (bf16[8,256,256]{2,1,0:T(8,128)(2,1)}, bf16[8,256,256]{2,1,0:T(8,128)(2,1)S(1)}, u32[]{:S(2)}) copy-start(bf16[8,256,256]{2,1,0:T(8,128)(2,1)S(1)} %all-to-all-done) | copy-start | bytes 3145732
  42.1 192.1 %all-to-all-start.1 = ((bf16[8,256,256]{1,2,0:T(8,128)(2,1)}), bf16[8,256,256]{1,2,0:T(8,128)(2,1)S(1)}, u32[]{:S(2)}, u32[]{:S(2)}) async-start(bf16[8,256,256]{1,2,0:T(8,128)(2,1)} %pad_maximum_fusion.2), calls=%async_computation.1 | async-start | bytes 2097152 | tf_op jit(solution)/shard_map/all_to_all | solution.py:1008
  49.0 441.9 %reduce-scatter.4.cloned.1.call-start = ((), (), s32[]{:S(2)}) async-start(), calls=%async_computation.8 | async-start | bytes 294912 | tf_op jit(solution)/shard_map/reduce_scatter | solution.py:1053
  50.6 54.6 %copy-start.16 = (bf16[256,32]{0,1:T(8,128)(2,1)S(1)}, bf16[256,32]{0,1:T(8,128)(2,1)}, u32[]{:S(2)}) copy-start(bf16[256,32]{0,1:T(8,128)(2,1)} %param.26) | copy-start | bytes 49156
  105.3 50.2 %copy-start.15 = (s32[2,128,8]{1,2,0:T(8,128)S(1)}, s32[2,128,8]{1,2,0:T(8,128)}, u32[]{:S(2)}) copy-start(s32[2,128,8]{1,2,0:T(8,128)} %param.17) | copy-start | bytes 24580
  215.2 7.2 copy-start.5
  234.7 4.7 copy-start.8
  280.0 1.8 copy-start.1
  421.9 56.3 %copy-start.3 = (bf16[2,128,2048]{2,1,0:T(8,128)(2,1)S(1)}, bf16[2,128,2048]{2,1,0:T(8,128)(2,1)}, u32[]{:S(2)}) copy-start(bf16[2,128,2048]{2,1,0:T(8,128)(2,1)} %multiply_convert_fusion.in_ref) | copy-start | bytes 3145732
  501.9 3.9 copy-start.4
  535.5 4.8 copy-start.6
  535.5 4.8 copy-start.9
  542.3 86.1 %all-to-all-start.3 = ((bf16[8,256,256]{2,1,0:T(8,128)(2,1)}), bf16[8,256,256]{2,1,0:T(8,128)(2,1)}, u32[]{:S(2)}, u32[]{:S(2)}) async-start(bf16[8,256,256]{2,1,0:T(8,128)(2,1)} %bitcast.102), calls=%async_computation.5 | async-start | bytes 2097152 | tf_op jit(solution)/shard_map/all_to_all | solution.py:1011
  547.9 189.2 %reduce-scatter.6.cloned.1.call-start = ((), (), s32[]{:S(2)}) async-start(), calls=%async_computation.9 | async-start | bytes 1179648 | tf_op jit(solution)/shard_map/reduce_scatter | solution.py:1094
  628.5 105.5 %all-to-all-start.2 = ((bf16[8,256,256]{2,1,0:T(8,128)(2,1)}), bf16[8,256,256]{2,1,0:T(8,128)(2,1)}, u32[]{:S(2)}, u32[]{:S(2)}) async-start(bf16[8,256,256]{2,1,0:T(8,128)(2,1)} %bitcast.93), calls=%async_computation.3 | async-start | bytes 2097152 | tf_op jit(solution)/shard_map/all_to_all | solution.py:1011
  634.7 153.9 %reduce-scatter.8.cloned.1.call-start = ((), (), s32[]{:S(2)}) async-start(), calls=%async_computation.10 | async-start | bytes 294912 | tf_op jit(solution)/shard_map/reduce_scatter | solution.py:1094
  641.1 42.3 %copy-start.17 = (f32[2,128]{1,0:T(2,128)S(1)}, f32[2,128]{1,0:T(2,128)}, u32[]{:S(2)}) copy-start(f32[2,128]{1,0:T(2,128)} %get-tuple-element.34) | copy-start | bytes 3076
  (3 other events, 4.6 us)
Sparse Core Ops, SparseCore 0:
  19.0 61.0 all-gather.1
  422.0 68.8 reduce-scatter.3
  566.4 68.9 reduce-scatter.5
  725.6 63.0 reduce-scatter.7

commit v2 on v1

--- a/solution.py
+++ b/solution.py
@@ -3,6 +3,7 @@
 
 import jax
 import jax.numpy as jnp
+import numpy as np
 from jax import lax
 from jax.experimental import pallas as pl
 from jax.experimental.pallas import tpu as pltpu
@@ -27,13 +28,30 @@
     return (2 * z + x, 2 * y + c)
 
 
-def greet(z, x, y, c):
-    barrier = pltpu.get_barrier_semaphore()
-    peers = [place(z, 1 - x, y, c), place(z, x, 1 - y, c), place(z, x, y, 1 - c)]
-    peers += [place((z + d) % 4, x, y, c) for d in (1, 2, 3)]
-    for peer in peers:
-        pl.semaphore_signal(barrier, inc=1, device_id=peer, device_id_type=MESH)
-    pl.semaphore_wait(barrier, len(peers))
+def span(first, count):
+    return pl.ds(pl.multiple_of(first, count), count)
+
+
+class Here:
+    def __init__(self):
+        z, x, y, c = coords()
+        self.z, self.x, self.y, self.c = z, x, y, c
+        self.f, self.t = 2 * z + x, 2 * y + c
+        self.xn, self.yn, self.cn = place(z, 1 - x, y, c), place(z, x, 1 - y, c), place(z, x, y, 1 - c)
+        self.lanes = ((x, y), (1 - x, y), (x, 1 - y), (1 - x, 1 - y))
+
+    def zd(self, d):
+        return (self.z + d) % 4
+
+    def peer(self, d, e):
+        return place(self.zd(d), (self.x + e) % 2, self.y, self.c)
+
+    def greet(self):
+        barrier = pltpu.get_barrier_semaphore()
+        peers = [self.peer(d, e) for d in range(4) for e in range(2) if d or e] + [self.yn, self.cn]
+        for peer in peers:
+            pl.semaphore_signal(barrier, inc=1, device_id=peer, device_id_type=MESH)
+        pl.semaphore_wait(barrier, len(peers))
 
 
 def push(src, dst, send_sem, recv_sem, device):
@@ -44,91 +62,105 @@
     return copy
 
 
-def landed(ref, sem, device):
-    pltpu.make_async_remote_copy(
-        src_ref=ref, dst_ref=ref, send_sem=sem, recv_sem=sem, device_id=device, device_id_type=MESH
-    ).wait_recv()
-
-
-def gather_kernel(whole, in_ref, out_ref, loc, sz, rz, sx, rx, sy, ry, sdx, rdx, sdy, rdy, sc, rc):
-    z, x, y, c = coords()
-    rows = in_ref.shape[1]
-    cols = in_ref.shape[2] // 4
-    half = rows // 2
-    f = 2 * z + x
-    t = 2 * y + c
-
-    def block(z_, x_, y_, c_, h=None):
-        first, count = ((2 * z_ + x_) * rows, rows) if h is None else ((2 * z_ + x_) * rows + h * half, half)
-        return out_ref.at[:, pl.ds(first, count), pl.ds((2 * y_ + c_) * cols, cols)]
-
-    def source(z_to, t_, first, count):
-        seqs = slice(None) if whole else pl.ds(z_to // 2, 1)
-        return in_ref.at[seqs, pl.ds(first, count), pl.ds(t_ * cols, cols)]
-
-    greet(z, x, y, c)
-    xn, yn, cn = place(z, 1 - x, y, c), place(z, x, 1 - y, c), place(z, x, y, 1 - c)
-    own_src = in_ref if whole else in_ref.at[pl.ds(z // 2, 1)]
-    own = pltpu.make_async_copy(own_src, out_ref.at[:, pl.ds(f * rows, rows), :], loc.at[0])
-    own.start()
-    order = (1, 3, 2)
-    sends = []
-    for d in order:
-        zd = (z + d) % 4
-        sends.append(push(source(zd, t, 0, rows), block(z, x, y, c), sz.at[d], rz.at[z], place(zd, x, y, c)))
-    sends.append(push(source(z, t, 0, rows), block(z, x, y, c), sx.at[z], rx.at[z], xn))
-    ty = 2 * (1 - y) + c
-    sends.append(push(source(z, ty, 0, half), block(z, x, 1 - y, c, 0), sdx.at[z], rdx.at[z], xn))
-    for d in order:
-        zd = (z + d) % 4
-        b = block(zd, x, y, c)
-        landed(b, rz.at[zd], xn)
-        sends.append(push(b, b, sx.at[zd], rx.at[zd], xn))
-        sends.append(push(b, b, sy.at[zd], ry.at[zd], yn))
-        sends.append(push(b, b, sc.at[0, zd], rc.at[0, zd], cn))
-    for d in (0,) + order:
-        zd = (z + d) % 4
-        b = block(zd, 1 - x, y, c)
-        landed(b, rx.at[zd], xn)
-        bh = block(zd, 1 - x, y, c, 1)
-        sends.append(push(bh, bh, sdy.at[zd], rdy.at[zd], yn))
-        sends.append(push(b, b, sc.at[1, zd], rc.at[1, zd], cn))
+def keep(src, dst, sem):
+    copy = pltpu.make_async_copy(src, dst, sem)
+    copy.start()
+    return copy
+
+
+ORDER = (1, 3, 2)
+FAR_FIRST = (2, 1, 3, 0)
+
+
+class Gather:
+    scratch = staticmethod(
+        lambda: [pltpu.SemaphoreType.DMA((1,))]
+        + [pltpu.SemaphoreType.DMA((4,))] * 10
+        + [pltpu.SemaphoreType.DMA((4, 4))] * 2
+    )
+    slots = 13
+
+    def __init__(self, here, whole, src, dst, sems):
+        self.here, self.whole, self.src, self.dst = here, whole, src, dst
+        (self.loc, self.sz, self.rz, self.sx, self.rx, self.sy, self.ry,
+         self.sdx, self.rdx, self.sdy, self.rdy, self.sc, self.rc) = sems
+        self.rows, self.cols = src.shape[1], src.shape[2] // 4
+        self.half = self.rows // 2
+        self.sends = []
+
+    def block(self, z, x, y, c, h=None):
+        first = (2 * z + x) * self.rows
+        rows = span(first, self.rows) if h is None else span(first + h * self.half, self.half)
+        return self.dst.at[:, rows, span((2 * y + c) * self.cols, self.cols)]
+
+    def source(self, z_to, t, first, count):
+        seqs = slice(None) if self.whole else pl.ds(z_to // 2, 1)
+        return self.src.at[seqs, pl.ds(first, count), span(t * self.cols, self.cols)]
+
+    def push(self, *args):
+        self.sends.append(push(*args))
+
+    def landed(self, ref, sem):
+        pltpu.make_async_remote_copy(
+            src_ref=ref, dst_ref=ref, send_sem=sem, recv_sem=sem, device_id=self.here.xn, device_id_type=MESH
+        ).wait_recv()
+
+    def start(self):
+        h = self.here
+        own = self.src if self.whole else self.src.at[pl.ds(h.z // 2, 1)]
+        self.own = keep(own, self.dst.at[:, span(h.f * self.rows, self.rows), :], self.loc.at[0])
+        for d in ORDER:
+            self.push(self.source(h.zd(d), h.t, 0, self.rows), self.block(h.z, h.x, h.y, h.c),
+                      self.sz.at[d], self.rz.at[h.z], h.peer(d, 0))
+        self.push(self.source(h.z, h.t, 0, self.rows), self.block(h.z, h.x, h.y, h.c),
+                  self.sx.at[h.z], self.rx.at[h.z], h.xn)
+        self.push(self.source(h.z, 2 * (1 - h.y) + h.c, 0, self.half), self.block(h.z, h.x, 1 - h.y, h.c, 0),
+                  self.sdx.at[h.z], self.rdx.at[h.z], h.xn)
+
+    def spread(self, d):
+        h, zd = self.here, self.here.zd(d)
+        b = self.block(zd, h.x, h.y, h.c)
+        self.landed(b, self.rz.at[zd])
+        self.push(b, b, self.sx.at[zd], self.rx.at[zd], h.xn)
+        self.push(b, b, self.sy.at[zd], self.ry.at[zd], h.yn)
+        self.push(b, b, self.sc.at[0, zd], self.rc.at[0, zd], h.cn)
+
+    def cross(self, d):
+        h, zd = self.here, self.here.zd(d)
+        b = self.block(zd, 1 - h.x, h.y, h.c)
+        self.landed(b, self.rx.at[zd])
+        low = self.block(zd, 1 - h.x, h.y, h.c, 1)
+        self.push(low, low, self.sdy.at[zd], self.rdy.at[zd], h.yn)
+        self.push(b, b, self.sc.at[1, zd], self.rc.at[1, zd], h.cn)
         if d != 0:
-            b = block(zd, x, 1 - y, c)
-            landed(b, ry.at[zd], xn)
-            bh = block(zd, x, 1 - y, c, 0)
-            sends.append(push(bh, bh, sdx.at[zd], rdx.at[zd], xn))
-            sends.append(push(b, b, sc.at[2, zd], rc.at[2, zd], cn))
-    for d in (0,) + order:
-        zd = (z + d) % 4
-        landed(block(zd, 1 - x, 1 - y, c, 0), rdx.at[zd], xn)
-        landed(block(zd, 1 - x, 1 - y, c, 1), rdy.at[zd], xn)
-        b = block(zd, 1 - x, 1 - y, c)
-        sends.append(push(b, b, sc.at[3, zd], rc.at[3, zd], cn))
-    for d in (0,) + order:
-        zd = (z + d) % 4
-        if d != 0:
-            landed(block(zd, x, y, 1 - c), rc.at[0, zd], xn)
-            landed(block(zd, x, 1 - y, 1 - c), rc.at[2, zd], xn)
-        landed(block(zd, 1 - x, y, 1 - c), rc.at[1, zd], xn)
-        landed(block(zd, 1 - x, 1 - y, 1 - c), rc.at[3, zd], xn)
-    for copy in sends:
-        copy.wait_send()
-    own.wait()
-
-
-def gather_rows(value, whole):
-    count, rows, width = value.shape
-    dma = pltpu.SemaphoreType.DMA
-    return pl.pallas_call(
-        functools.partial(gather_kernel, whole),
-        out_shape=jax.ShapeDtypeStruct((count if whole else 1, rows * 8, width), value.dtype),
-        in_specs=[pl.BlockSpec(memory_space=pl.ANY)],
-        out_specs=pl.BlockSpec(memory_space=pl.ANY),
-        scratch_shapes=[dma((1,))] + [dma((4,))] * 10 + [dma((4, 4))] * 2,
-        compiler_params=pltpu.CompilerParams(collective_id=0 if whole else 1, has_side_effects=True),
-        name="gather_whole" if whole else "gather_half",
-    )(value)
+            b = self.block(zd, h.x, 1 - h.y, h.c)
+            self.landed(b, self.ry.at[zd])
+            top = self.block(zd, h.x, 1 - h.y, h.c, 0)
+            self.push(top, top, self.sdx.at[zd], self.rdx.at[zd], h.xn)
+            self.push(b, b, self.sc.at[2, zd], self.rc.at[2, zd], h.cn)
+
+    def close(self, d):
+        h, zd = self.here, self.here.zd(d)
+        self.landed(self.block(zd, 1 - h.x, 1 - h.y, h.c, 0), self.rdx.at[zd])
+        self.landed(self.block(zd, 1 - h.x, 1 - h.y, h.c, 1), self.rdy.at[zd])
+        b = self.block(zd, 1 - h.x, 1 - h.y, h.c)
+        self.push(b, b, self.sc.at[3, zd], self.rc.at[3, zd], h.cn)
+
+    def arrived(self, d, e):
+        h, zd = self.here, self.here.zd(d)
+        if e == 0:
+            if d == 0:
+                self.own.wait()
+            else:
+                self.landed(self.block(zd, h.x, h.y, 1 - h.c), self.rc.at[0, zd])
+                self.landed(self.block(zd, h.x, 1 - h.y, 1 - h.c), self.rc.at[2, zd])
+        else:
+            self.landed(self.block(zd, 1 - h.x, h.y, 1 - h.c), self.rc.at[1, zd])
+            self.landed(self.block(zd, 1 - h.x, 1 - h.y, 1 - h.c), self.rc.at[3, zd])
+
+    def finish(self):
+        for copy in self.sends:
+            copy.wait_send()
 
 
 def add_into(target, *others):
@@ -145,110 +177,15 @@
         target[n, r, :] = total.astype(target.dtype)
 
 
-def sum_kernel(whole, in_ref, out_ref, acc, fc, f1x, f1y, f2x, f2y, fz, full, tmp,
-               lsem, sc, rc, s1x, r1x, s1y, r1y, s2x, r2x, s2y, r2y, sz, rz, sg, rg, osem):
-    z, x, y, c = coords()
-    rows = out_ref.shape[1]
-    cols = out_ref.shape[2] // 4
-    half = rows // 2
-    xn, yn, cn = place(z, 1 - x, y, c), place(z, x, 1 - y, c), place(z, x, y, 1 - c)
-    lanes = ((x, y), (1 - x, y), (x, 1 - y), (1 - x, 1 - y))
-
-    def block(z_, lane, c_):
-        x_, y_ = lanes[lane]
-        return in_ref.at[:, pl.ds((2 * z_ + x_) * rows, rows), pl.ds((2 * y_ + c_) * cols, cols)]
-
-    greet(z, x, y, c)
-    sends = []
-    loads = {}
-    order = (2, 1, 3, 0)
-    for lane in (3, 1, 2, 0):
-        for d in order:
-            zd = (z + d) % 4
-            sends.append(push(block(zd, lane, 1 - c), fc.at[lane, d], sc.at[lane, d], rc.at[lane, d], cn))
-            loads[lane, d] = pltpu.make_async_copy(block(zd, lane, c), acc.at[lane, d], lsem.at[lane, d])
-            loads[lane, d].start()
-
-    def core_sum(lane, d):
-        loads[lane, d].wait()
-        landed(fc.at[lane, d], rc.at[lane, d], cn)
-        add_into(acc.at[lane, d], fc.at[lane, d])
-
-    top, low = pl.ds(0, half), pl.ds(half, half)
-    for d in order:
-        core_sum(3, d)
-        sends.append(push(acc.at[3, d, :, top], f1x.at[d], s1x.at[d], r1x.at[d], xn))
-        sends.append(push(acc.at[3, d, :, low], f1y.at[d], s1y.at[d], r1y.at[d], yn))
-    for d in order:
-        core_sum(1, d)
-        core_sum(2, d)
-        landed(f1y.at[d], r1y.at[d], yn)
-        add_into(acc.at[1, d, :, low], f1y.at[d])
-        sends.append(push(acc.at[1, d], f2x.at[d], s2x.at[d], r2x.at[d], xn))
-        landed(f1x.at[d], r1x.at[d], xn)
-        add_into(acc.at[2, d, :, top], f1x.at[d])
-        sends.append(push(acc.at[2, d], f2y.at[d], s2y.at[d], r2y.at[d], yn))
-    for d in order:
-        core_sum(0, d)
-        landed(f2x.at[d], r2x.at[d], xn)
-        landed(f2y.at[d], r2y.at[d], yn)
-        add_into(acc.at[0, d], f2x.at[d], f2y.at[d])
-        if d != 0:
-            zd = (z + d) % 4
-            sends.append(push(acc.at[0, d], fz.at[(4 - d) % 4], sz.at[d], rz.at[(4 - d) % 4], place(zd, x, y, c)))
-    t = 2 * y + c
-    for d in (1, 2, 3):
-        landed(fz.at[d], rz.at[d], cn)
-    step = 32
-
-    @pl.loop(0, 2 * rows // step)
-    def _(i):
-        n = i // (rows // step)
-        r = pl.ds(pl.multiple_of((i % (rows // step)) * step, step), step)
-        if whole:
-            total = acc[0, 0, n, r, :].astype(F32)
-            for d in (1, 2, 3):
-                total = total + fz[d, n, r, :].astype(F32)
-        else:
-            total = jnp.where(z // 2 == n, acc[0, 0, 0, r, :].astype(F32), 0.0)
-            for d in (1, 2, 3):
-                total = total + jnp.where(((z + d) % 4) // 2 == n, fz[d, 0, r, :].astype(F32), 0.0)
-        tmp[n, r, :] = total.astype(tmp.dtype)
-
-    mine = full.at[t]
-    keep = pltpu.make_async_copy(tmp, mine, osem.at[4])
-    keep.start()
-    sends.append(push(tmp, mine, sg.at[0], rg.at[0], yn))
-    sends.append(push(tmp, mine, sg.at[1], rg.at[1], cn))
-    ty, tc, td = 2 * (1 - y) + c, 2 * y + 1 - c, 2 * (1 - y) + 1 - c
-    landed(full.at[ty], rg.at[0], yn)
-    sends.append(push(full.at[ty], full.at[ty], sg.at[2], rg.at[2], cn))
-    landed(full.at[tc], rg.at[1], cn)
-    landed(full.at[td], rg.at[2], cn)
-    keep.wait()
-    outs = []
-    for q in range(4):
-        outs.append(pltpu.make_async_copy(full.at[q], out_ref.at[:, :, pl.ds(q * cols, cols)], osem.at[q]))
-        outs[-1].start()
-    for copy in sends:
-        copy.wait_send()
-    for copy in outs:
-        copy.wait()
-
-
-def sum_rows(value, whole):
-    count, total_rows, width = value.shape
-    rows, cols = total_rows // 8, width // 4
-    dma = pltpu.SemaphoreType.DMA
-    low = value.dtype
-    vm = pltpu.VMEM
-    return pl.pallas_call(
-        functools.partial(sum_kernel, whole),
-        out_shape=jax.ShapeDtypeStruct((2, rows, width), low),
-        in_specs=[pl.BlockSpec(memory_space=pl.ANY)],
-        out_specs=pl.BlockSpec(memory_space=pl.ANY),
-        scratch_shapes=[
-            vm((4, 4, count, rows, cols), low),
+class Sum:
+    slots = 24
+
+    @staticmethod
+    def scratch(count, rows, width, low):
+        dma = pltpu.SemaphoreType.DMA
+        cols = width // 4
+        vm = pltpu.VMEM
+        return [
             vm((4, 4, count, rows, cols), low),
             vm((4, count, rows // 2, cols), low),
             vm((4, count, rows // 2, cols), low),
@@ -257,8 +194,142 @@
             vm((4, count, rows, cols), low),
             vm((4, 2, rows, cols), low),
             vm((2, rows, cols), low),
-            dma((4, 4)), dma((4, 4)), dma((4, 4)),
-        ] + [dma((4,))] * 10 + [dma((3,))] * 2 + [dma((5,))],
+            vm((2, rows, cols), F32),
+            dma((4, 4)), dma((4, 4)),
+        ] + [dma((4,))] * 10 + [dma((3,))] * 2 + [dma((5,))]
+
+    def __init__(self, here, whole, part, refs):
+        self.here, self.whole, self.part = here, whole, part
+        (self.fc, self.f1x, self.f1y, self.f2x, self.f2y, self.fz, self.full, self.tmp, self.wide, self.sc, self.rc,
+         self.s1x, self.r1x, self.s1y, self.r1y, self.s2x, self.r2x, self.s2y, self.r2y, self.sz, self.rz,
+         self.sg, self.rg, self.osem) = refs
+        self.rows, self.cols = part.shape[1] // 8, part.shape[2] // 4
+        self.top, self.low = pl.ds(0, self.rows // 2), pl.ds(self.rows // 2, self.rows // 2)
+        self.sends = []
+
+    def block(self, d, lane, c):
+        x, y = self.here.lanes[lane]
+        return self.part.at[:, span((2 * self.here.zd(d) + x) * self.rows, self.rows),
+                            span((2 * y + c) * self.cols, self.cols)]
+
+    def push(self, *args):
+        self.sends.append(push(*args))
+
+    def landed(self, ref, sem):
+        pltpu.make_async_remote_copy(
+            src_ref=ref, dst_ref=ref, send_sem=sem, recv_sem=sem, device_id=self.here.xn, device_id_type=MESH
+        ).wait_recv()
+
+    def give(self, d, e):
+        for lane in ((1, 3) if e else (0, 2)):
+            self.push(self.block(d, lane, 1 - self.here.c), self.fc.at[lane, d],
+                      self.sc.at[lane, d], self.rc.at[lane, d], self.here.cn)
+
+    def pair(self, lane, d):
+        self.landed(self.fc.at[lane, d], self.rc.at[lane, d])
+        add_into(self.block(d, lane, self.here.c), self.fc.at[lane, d])
+        return self.block(d, lane, self.here.c)
+
+    def corner(self, d):
+        b = self.pair(3, d)
+        self.push(b.at[:, self.top], self.f1x.at[d], self.s1x.at[d], self.r1x.at[d], self.here.xn)
+        self.push(b.at[:, self.low], self.f1y.at[d], self.s1y.at[d], self.r1y.at[d], self.here.yn)
+
+    def sides(self, d):
+        b = self.pair(1, d)
+        self.landed(self.f1y.at[d], self.r1y.at[d])
+        add_into(b.at[:, self.low], self.f1y.at[d])
+        self.push(b, self.f2x.at[d], self.s2x.at[d], self.r2x.at[d], self.here.xn)
+        b = self.pair(2, d)
+        self.landed(self.f1x.at[d], self.r1x.at[d])
+        add_into(b.at[:, self.top], self.f1x.at[d])
+        self.push(b, self.f2y.at[d], self.s2y.at[d], self.r2y.at[d], self.here.yn)
+
+    def centre(self, d):
+        b = self.pair(0, d)
+        self.landed(self.f2x.at[d], self.r2x.at[d])
+        self.landed(self.f2y.at[d], self.r2y.at[d])
+        add_into(b, self.f2x.at[d], self.f2y.at[d])
+        if d != 0:
+            self.push(b, self.fz.at[(4 - d) % 4], self.sz.at[d], self.rz.at[(4 - d) % 4], self.here.peer(d, 0))
+
+    def total(self):
+        for d in (1, 2, 3):
+            self.landed(self.fz.at[d], self.rz.at[d])
+        b = self.block(0, 0, self.here.c)
+        step = 32
+
+        @pl.loop(0, 2 * self.rows // step)
+        def _(i):
+            n = i // (self.rows // step)
+            r = pl.ds(pl.multiple_of((i % (self.rows // step)) * step, step), step)
+            if self.whole:
+                total = b[n, r, :].astype(F32)
+                for d in (1, 2, 3):
+                    total = total + self.fz[d, n, r, :].astype(F32)
+            else:
+                total = jnp.where(self.here.z // 2 == n, b[0, r, :].astype(F32), 0.0)
+                for d in (1, 2, 3):
+                    total = total + jnp.where(self.here.zd(d) // 2 == n, self.fz[d, 0, r, :].astype(F32), 0.0)
+            self.tmp[n, r, :] = total.astype(self.tmp.dtype)
+
+    def share(self, out):
+        h = self.here
+        mine = self.full.at[h.t]
+        self.keeps = [keep(self.tmp, mine, self.osem.at[4])]
+        self.push(self.tmp, mine, self.sg.at[0], self.rg.at[0], h.yn)
+        self.push(self.tmp, mine, self.sg.at[1], self.rg.at[1], h.cn)
+        ty, tc, td = 2 * (1 - h.y) + h.c, 2 * h.y + 1 - h.c, 2 * (1 - h.y) + 1 - h.c
+        self.landed(self.full.at[ty], self.rg.at[0])
+        self.push(self.full.at[ty], self.full.at[ty], self.sg.at[2], self.rg.at[2], h.cn)
+        self.landed(self.full.at[tc], self.rg.at[1])
+        self.landed(self.full.at[td], self.rg.at[2])
+        self.keeps[0].wait()
+        outs = [keep(self.full.at[q], out.at[:, :, pl.ds(q * self.cols, self.cols)], self.osem.at[q]) for q in range(4)]
+        for copy in outs:
+            copy.wait()
+
+    def finish(self):
+        for copy in self.sends:
+            copy.wait_send()
+
+
+def sum_kernel(whole, in_ref, out_ref, part, load, *refs):
+    here = Here()
+    here.greet()
+    total = Sum(here, whole, part, refs)
+    rows = total.rows
+    copies = {}
+    for e in (1, 0):
+        for d in FAR_FIRST:
+            at = span((2 * here.zd(d) + (here.x + e) % 2) * rows, rows)
+            copies[d, e] = keep(in_ref.at[:, at, :], part.at[:, at, :], load.at[e, d])
+    for e in (1, 0):
+        for d in FAR_FIRST:
+            copies[d, e].wait()
+            total.give(d, e)
+    for d in FAR_FIRST:
+        total.corner(d)
+    for d in FAR_FIRST:
+        total.sides(d)
+    for d in FAR_FIRST:
+        total.centre(d)
+    total.total()
+    total.share(out_ref)
+    total.finish()
+
+
+def sum_rows(value, whole):
+    count, total_rows, width = value.shape
+    rows = total_rows // 8
+    low = value.dtype
+    return pl.pallas_call(
+        functools.partial(sum_kernel, whole),
+        out_shape=jax.ShapeDtypeStruct((2, rows, width), low),
+        in_specs=[pl.BlockSpec(memory_space=pl.ANY)],
+        out_specs=pl.BlockSpec(memory_space=pl.ANY),
+        scratch_shapes=[pltpu.VMEM((count, total_rows, width), low), pltpu.SemaphoreType.DMA((2, 4))]
+        + Sum.scratch(count, rows, width, low),
         compiler_params=pltpu.CompilerParams(
             collective_id=2 if whole else 3, has_side_effects=True, vmem_limit_bytes=VMEM_LIMIT
         ),
@@ -266,6 +337,47 @@
     )(value)
 
 
+def gather_kernel(whole, in_ref, out_ref, *sems):
+    here = Here()
+    here.greet()
+    rows = Gather(here, whole, in_ref, out_ref, sems)
+    rows.start()
+    for d in ORDER:
+        rows.spread(d)
+    for d in (0,) + ORDER:
+        rows.cross(d)
+    for d in (0,) + ORDER:
+        rows.close(d)
+    for d in (0,) + ORDER:
+        rows.arrived(d, 0)
+        rows.arrived(d, 1)
+    rows.finish()
+
+
+def gather_rows(value, whole):
+    count, rows, width = value.shape
+    return pl.pallas_call(
+        functools.partial(gather_kernel, whole),
+        out_shape=jax.ShapeDtypeStruct((count if whole else 1, rows * 8, width), value.dtype),
+        in_specs=[pl.BlockSpec(memory_space=pl.ANY)],
+        out_specs=pl.BlockSpec(memory_space=pl.ANY),
+        scratch_shapes=Gather.scratch(),
+        compiler_params=pltpu.CompilerParams(collective_id=0 if whole else 1, has_side_effects=True),
+        name="gather_whole" if whole else "gather_half",
+    )(value)
+
+
+def signed_tables(length, width):
+    middle = width // 2
+    frequency = rope_base ** (-np.arange(middle) * 2.0 / width)
+    angles = np.arange(length)[:, None] * frequency[None, :]
+    cosine, sine = np.cos(angles), np.sin(angles)
+    return (
+        jnp.asarray(np.concatenate([cosine, cosine], axis=1), F32),
+        jnp.asarray(np.concatenate([-sine, sine], axis=1), F32),
+    )
+
+
 def dot_nn(a, b):
     return jnp.dot(a, b, preferred_element_type=F32)
 
@@ -276,65 +388,6 @@
 
 def dot_tn(a, b):
     return lax.dot_general(a, b, (((0,), (0,)), ((), ())), preferred_element_type=F32)
-
-
-def turn_half(values):
-    width = values.shape[-1]
-    lane = lax.broadcasted_iota(jnp.int32, values.shape, values.ndim - 1)
-    rolled = pltpu.roll(values, width // 2, values.ndim - 1)
-    return jnp.where(lane < width // 2, -rolled, rolled)
-
-
-def attend_kernel(heads, xn_ref, w_ref, cos_ref, sin_ref, qg_ref, kg_ref,
-                  pre_ref, qkv_ref, prob_ref, ctx_ref):
-    seq = xn_ref.shape[0]
-    hd = cos_ref.shape[1]
-    tile = 256
-    scale = 1.0 / math.sqrt(hd)
-    for i in range(seq // tile):
-        r = pl.ds(i * tile, tile)
-        pre = dot_nn(xn_ref[r, :], w_ref[...])
-        pre_ref[r, :] = pre[:, : (heads + 1) * hd]
-        qkv_ref[r, pl.ds((heads + 1) * hd, hd)] = pre[:, (heads + 1) * hd :].astype(LOW)
-        for a in range(heads + 1):
-            one = pre[:, a * hd : (a + 1) * hd]
-            factor = lax.rsqrt(jnp.mean(one * one, axis=-1, keepdims=True) + norm_eps)
-            gained = one * factor * (qg_ref if a < heads else kg_ref)[...]
-            turned = gained * cos_ref[r, :] + turn_half(gained) * sin_ref[r, :]
-            qkv_ref[r, pl.ds(a * hd, hd)] = turned.astype(LOW)
-    for a in range(heads):
-        for i in range(seq // tile):
-            r = pl.ds(i * tile, tile)
-            n = (i + 1) * tile
-            query = qkv_ref[r, pl.ds(a * hd, hd)]
-            key = qkv_ref[pl.ds(0, n), pl.ds(heads * hd, hd)]
-            value = qkv_ref[pl.ds(0, n), pl.ds((heads + 1) * hd, hd)]
-            score = dot_nt(query, key) * scale
-            row = lax.broadcasted_iota(jnp.int32, (tile, n), 0) + i * tile
-            col = lax.broadcasted_iota(jnp.int32, (tile, n), 1)
-            score = jnp.where(col <= row, score, masked_score)
-            peak = jnp.max(score, axis=-1, keepdims=True)
-            terms = jnp.exp(score - peak)
-            prob = (terms * (1.0 / jnp.sum(terms, axis=-1, keepdims=True))).astype(LOW)
-            prob_ref[a, r, pl.ds(0, n)] = prob
-            ctx_ref[r, pl.ds(a * hd, hd)] = dot_nn(prob, value).astype(LOW)
-
-
-def attend(xn, weights, cosine, sine, query_gain, key_gain):
-    seq = xn.shape[0]
-    hd = query_gain.shape[0]
-    heads = weights.shape[1] // hd - 2
-    return pl.pallas_call(
-        functools.partial(attend_kernel, heads),
-        out_shape=(
-            jax.ShapeDtypeStruct((seq, (heads + 1) * hd), F32),
-            jax.ShapeDtypeStruct((seq, (heads + 2) * hd), LOW),
-            jax.ShapeDtypeStruct((heads, seq, seq), LOW),
-            jax.ShapeDtypeStruct((seq, heads * hd), LOW),
-        ),
-        compiler_params=pltpu.CompilerParams(vmem_limit_bytes=VMEM_LIMIT),
-        name="attend",
-    )(xn, weights, cosine, sine, query_gain[None], key_gain[None])
 
 
 def attend_back_kernel(heads, dctx_ref, pre_ref, qkv_ref, prob_ref, cos_ref, sin_ref, qg_ref, kg_ref,
@@ -371,7 +424,7 @@
             one = pre_ref[r, pl.ds(a * hd, hd)]
             factor = lax.rsqrt(jnp.mean(one * one, axis=-1, keepdims=True) + norm_eps)
             hat = one * factor
-            turned = up * cos_ref[r, :] - turn_half(up * sin_ref[r, :])
+            turned = up * cos_ref[r, :] + pltpu.roll(up * sin_ref[r, :], hd // 2, 1)
             part = jnp.sum(turned * hat, axis=0, keepdims=True)
             gained = turned * (qg_ref if a < heads else kg_ref)[...]
             back = factor * (gained - hat * jnp.mean(gained * hat, axis=-1, keepdims=True))
@@ -517,6 +570,221 @@
     )(first, x, og, ids, router, gate.reshape(hidden, width), up.reshape(hidden, width), down.reshape(hidden, width))
 
 
+class Weights:
+    scratch = staticmethod(lambda: [pltpu.SemaphoreType.DMA((8, 4, 2))] * 4 + [pltpu.SemaphoreType.DMA((6,))])
+    slots = 5
+
+    def __init__(self, here, query, key, value, output, router, ids, w, wo, router_all, ids_all, sems):
+        self.here = here
+        self.query, self.output, self.w, self.wo = query, output, w, wo
+        piece, part = query.shape[0], wo.shape[1]
+        self.piece, self.part = piece, part
+        hd = key.shape[1]
+        self.shared = (
+            (key, lambda f: w.at[span(f * piece, piece), pl.ds(part, hd)]),
+            (value, lambda f: w.at[span(f * piece, piece), pl.ds(part + hd, hd)]),
+            (router, lambda f: router_all.at[:, span(f * piece, piece)]),
+            (ids, lambda f: ids_all.at[:, :, span(f * ids.shape[2], ids.shape[2])]),
+        )
+        self.qs, self.qr, self.ss, self.sr, self.loc = sems
+        self.sends, self.keeps = [], []
+
+    def landed(self, ref, sem):
+        pltpu.make_async_remote_copy(
+            src_ref=ref, dst_ref=ref, send_sem=sem, recv_sem=sem, device_id=self.here.xn, device_id_type=MESH
+        ).wait_recv()
+
+    def start_shared(self):
+        h = self.here
+        for n, (src, dst) in enumerate(self.shared):
+            self.keeps.append(keep(src, dst(h.f), self.loc.at[n]))
+            for d, e in ((2, 0), (1, 0), (3, 0), (0, 1)):
+                self.sends.append(push(src, dst(h.f), self.ss.at[n, d, e], self.sr.at[n, (4 - d) % 4, e], h.peer(d, e)))
+
+    def pass_shared(self, d):
+        h = self.here
+        for n, (_, dst) in enumerate(self.shared):
+            ref = dst(2 * h.zd(d) + h.x)
+            self.landed(ref, self.sr.at[n, d, 0])
+            self.sends.append(push(ref, ref, self.ss.at[n, d, 1], self.sr.at[n, d, 1], h.xn))
+
+    def wait_shared(self):
+        h = self.here
+        for n, (_, dst) in enumerate(self.shared):
+            for d in range(4):
+                self.landed(dst(2 * h.zd(d) + 1 - h.x), self.sr.at[n, d, 1])
+
+    def start_pairs(self, n):
+        h = self.here
+        src, dst = ((self.query, self.w), (self.output, self.wo))[n]
+        mine = lambda f: dst.at[span(f * self.piece, self.piece), pl.ds(0, self.part)]
+        self.keeps.append(keep(src.at[:, span((h.f % 4) * self.part, self.part)], mine(h.f), self.loc.at[4 + n]))
+        for d in FAR_FIRST:
+            for e in (1, 0):
+                if d or e:
+                    f = 2 * h.zd(d) + (h.x + e) % 2
+                    self.sends.append(push(src.at[:, span((f % 4) * self.part, self.part)], mine(h.f),
+                                           self.qs.at[n, d, e], self.qr.at[n, (4 - d) % 4, e], h.peer(d, e)))
+
+    def wait_pairs(self, n):
+        h = self.here
+        dst = (self.w, self.wo)[n]
+        for d in range(4):
+            for e in (1, 0):
+                if d or e:
+                    f = 2 * h.zd(d) + (h.x + e) % 2
+                    self.landed(dst.at[span(f * self.piece, self.piece), pl.ds(0, self.part)], self.qr.at[n, d, e])
+
+    def finish(self):
+        for copy in self.sends:
+            copy.wait_send()
+
+
+def begin_kernel(heads, normed, cot, query, key, value, output, router, ids, cos_ref, sin_ref, qg_ref, kg_ref,
+                 xn_out, w_out, wo_out, router_out, ids_out, cot_out, pre_out, qkv_out, prob_out, ctx_out, branch_out,
+                 xn, w, wo, pre, qkv, prob, ctx, part, osem, *sems):
+    here = Here()
+    here.greet()
+    at = 0
+    x_rows = Gather(here, False, normed, xn, sems[at : at + Gather.slots])
+    at += Gather.slots
+    c_rows = Gather(here, True, cot, cot_out, sems[at : at + Gather.slots])
+    at += Gather.slots
+    moved = Weights(here, query, key, value, output, router, ids, w, wo, router_out, ids_out, sems[at : at + Weights.slots])
+    at += Weights.slots
+    total = Sum(here, False, part, sems[at:])
+
+    x_rows.start()
+    moved.start_shared()
+    moved.start_pairs(0)
+    for d in ORDER:
+        x_rows.spread(d)
+        moved.pass_shared(d)
+    for d in (0,) + ORDER:
+        x_rows.cross(d)
+    for d in (0,) + ORDER:
+        x_rows.close(d)
+    for d in (0,) + ORDER:
+        x_rows.arrived(d, 0)
+        x_rows.arrived(d, 1)
+    moved.wait_shared()
+    moved.wait_pairs(0)
+    for copy in moved.keeps:
+        copy.wait()
+    c_rows.start()
+    moved.keeps = []
+    moved.start_pairs(1)
+    outs = [keep(xn, xn_out, osem.at[0]), keep(w, w_out, osem.at[1])]
+
+    seq = xn.shape[1]
+    hd = cos_ref.shape[1]
+    tile = 256
+    scale = 1.0 / math.sqrt(hd)
+    for i in range(seq // tile):
+        r = pl.ds(i * tile, tile)
+        got = dot_nn(xn[0, r, :], w[...])
+        pre[r, :] = got[:, : (heads + 1) * hd]
+        qkv[r, pl.ds((heads + 1) * hd, hd)] = got[:, (heads + 1) * hd :].astype(LOW)
+        for a in range(heads + 1):
+            one = got[:, a * hd : (a + 1) * hd]
+            factor = lax.rsqrt(jnp.mean(one * one, axis=-1, keepdims=True) + norm_eps)
+            gained = one * factor * (qg_ref if a < heads else kg_ref)[...]
+            turned = gained * cos_ref[r, :] + pltpu.roll(gained, hd // 2, 1) * sin_ref[r, :]
+            qkv[r, pl.ds(a * hd, hd)] = turned.astype(LOW)
+    outs += [keep(pre, pre_out, osem.at[2]), keep(qkv, qkv_out, osem.at[3])]
+    for d in ORDER:
+        c_rows.spread(d)
+    for a in range(heads):
+        for i in range(seq // tile):
+            r = pl.ds(i * tile, tile)
+            n = (i + 1) * tile
+            score = dot_nt(qkv[r, pl.ds(a * hd, hd)], qkv[pl.ds(0, n), pl.ds(heads * hd, hd)]) * scale
+            row = lax.broadcasted_iota(jnp.int32, (tile, n), 0) + i * tile
+            col = lax.broadcasted_iota(jnp.int32, (tile, n), 1)
+            score = jnp.where(col <= row, score, masked_score)
+            terms = jnp.exp(score - jnp.max(score, axis=-1, keepdims=True))
+            low = (terms * (1.0 / jnp.sum(terms, axis=-1, keepdims=True))).astype(LOW)
+            prob[a, r, pl.ds(0, n)] = low
+            ctx[r, pl.ds(a * hd, hd)] = dot_nn(low, qkv[pl.ds(0, n), pl.ds((heads + 1) * hd, hd)]).astype(LOW)
+        if a == 0:
+            for d in (0,) + ORDER:
+                c_rows.cross(d)
+    outs += [keep(prob, prob_out, osem.at[4]), keep(ctx, ctx_out, osem.at[5])]
+    moved.wait_pairs(1)
+    for copy in moved.keeps:
+        copy.wait()
+    outs.append(keep(wo, wo_out, osem.at[6]))
+    rows = total.rows
+    for e in (1, 0):
+        for d in FAR_FIRST:
+            at_f = span((2 * here.zd(d) + (here.x + e) % 2) * rows, rows)
+            part[0, at_f, :] = dot_nt(ctx[at_f, :], wo[...]).astype(LOW)
+            total.give(d, e)
+    for d in FAR_FIRST:
+        total.corner(d)
+    for d in (0,) + ORDER:
+        c_rows.close(d)
+    for d in FAR_FIRST:
+        total.sides(d)
+    for d in FAR_FIRST:
+        total.centre(d)
+    total.total()
+    total.share(branch_out)
+    for d in (0,) + ORDER:
+        c_rows.arrived(d, 0)
+        c_rows.arrived(d, 1)
+    for each in (x_rows, c_rows, moved, total):
+        each.finish()
+    for copy in outs:
+        copy.wait()
+
+
+def begin(normed, cot, query, key, value, output, router, ids, cosine, sine, query_gain, key_gain):
+    count, rows, width = normed.shape
+    seq = rows * 8
+    hd = query_gain.shape[0]
+    part = query.shape[1] // 4
+    heads = part // hd
+    vm = pltpu.VMEM
+    hbm = pl.BlockSpec(memory_space=pl.ANY)
+    near = pl.BlockSpec(memory_space=pltpu.VMEM)
+    shape = jax.ShapeDtypeStruct
+    local = [
+        ((1, seq, width), LOW),
+        ((width, part + 2 * hd), LOW),
+        ((width, part), LOW),
+        ((seq, (heads + 1) * hd), F32),
+        ((seq, (heads + 2) * hd), LOW),
+        ((heads, seq, seq), LOW),
+        ((seq, heads * hd), LOW),
+    ]
+    return pl.pallas_call(
+        functools.partial(begin_kernel, heads),
+        out_shape=(
+            shape(*local[0]),
+            shape(*local[1]),
+            shape(*local[2]),
+            shape((router.shape[0], width), LOW),
+            shape((count, ids.shape[1], seq), jnp.int32),
+            shape((count, seq, width), LOW),
+            shape(*local[3]),
+            shape(*local[4]),
+            shape(*local[5]),
+            shape(*local[6]),
+            shape((count, rows, width), LOW),
+        ),
+        in_specs=[hbm] * 8 + [near] * 4,
+        out_specs=[hbm] * 11,
+        scratch_shapes=[vm(*entry) for entry in local]
+        + [vm((1, seq, width), LOW), pltpu.SemaphoreType.DMA((7,))]
+        + Gather.scratch() + Gather.scratch() + Weights.scratch() + Sum.scratch(1, rows, width, LOW),
+        compiler_params=pltpu.CompilerParams(
+            collective_id=4, has_side_effects=True, vmem_limit_bytes=VMEM_LIMIT
+        ),
+        name="begin",
+    )(normed, cot, query, key, value, output, router, ids, cosine, sine, query_gain[None], key_gain[None])
+
+
 def rotate_half(values):
     middle = values.shape[-1] // 2
     return jnp.concatenate([-values[..., middle:], values[..., :middle]], axis=-1)
@@ -997,15 +1265,10 @@
     part = local // pairs
     piece = query_weight.shape[0]
 
-    cosine, sine = rope_tables(jnp.arange(seq, dtype=jnp.int32), hd)
+    cosine, sine = signed_tables(seq, hd)
     inputs = tokens.astype(F32)
     input_hat, attention_factor = norm_parts(inputs)
     normed = (input_hat * attention_gain).astype(LOW)
-
-    def fetch(weight):
-        cut = weight.reshape(piece, pairs, part).transpose(1, 0, 2)
-        cut = jnp.concatenate([cut] * count, axis=0)
-        return lax.all_to_all(cut, "fsdp", split_axis=0, concat_axis=0, tiled=True).reshape(width, part)
 
     def give_back(grad):
         cut = lax.all_to_all(
@@ -1014,34 +1277,35 @@
         cut = jnp.sum(cut.reshape(count, pairs, piece, part), axis=0)
         return cut.transpose(1, 0, 2).reshape(piece, local)
 
-    query_pair = fetch(query_weight)
-    output_pair = fetch(output_weight)
-    key_value = lax.all_gather(
-        jnp.concatenate([key_weight, value_weight], axis=1), "fsdp", axis=0, tiled=True
+    (normed_all, weights, output_pair, router_all, ids_all, grad_all, pre, qkv, prob, context, branch) = begin(
+        normed,
+        cotangent,
+        query_weight,
+        key_weight,
+        value_weight,
+        output_weight,
+        router_weight.T,
+        expert_ids.transpose(0, 2, 1),
+        cosine,
+        sine,
+        query_gain,
+        key_gain,
     )
-    router_full = lax.all_gather(router_weight, "fsdp", axis=0, tiled=True)
-    ids_all = lax.all_gather(expert_ids, "fsdp", axis=1, tiled=True)
-
-    normed_all = gather_rows(normed, False)[0]
-    weights = jnp.concatenate([query_pair, key_value], axis=1)
-    pre, qkv, prob, context = attend(normed_all, weights, cosine, sine, query_gain, key_gain)
-    branch_part = lax.dot_general(
-        context, output_pair, (((1,), (1,)), ((), ())), preferred_element_type=F32
-    ).astype(LOW)
-    branch = sum_rows(branch_part[None], False)
+    normed_all = normed_all[0]
+    router_full = router_all.T
+    ids_all = ids_all.transpose(0, 2, 1)
     resid = inputs + branch.astype(F32)
     resid_hat, expert_factor = norm_parts(resid)
     expert_in = (resid_hat * expert_gain).astype(LOW)
 
     expert_all = gather_rows(expert_in, True).reshape(count * seq, width)
-    grad_all = gather_rows(cotangent, True).reshape(count * seq, width)
     lanes = 128
     router_wide = jnp.pad(router_full, ((0, 0), (0, lanes - expert_count)))
     first = (f * experts).astype(jnp.int32).reshape(1)
     out_part, dx_part, dgp_part, d_gate, d_up, d_down = run_experts(
         first,
         expert_all,
-        grad_all,
+        grad_all.reshape(count * seq, width),
         ids_all.reshape(count * seq, -1),
         router_wide,
         gate_weight,

time: 802 us -> 687 us (0.86)
  blocking collectives: 106 us -> 47.3 us
  waiting for transfers between devices: 85.7 us -> 58.1 us
  starting transfers between devices: 25 us -> 10.7 us
    pallas_call x1, Pallas kernels: 11.8 us -> 144 us  [begin(): pl.pallas_call(functools.partial(begin_kernel, heads), out_shape=(shape(*...]
    pallas_call x4 -> x2, Pallas kernels: 182 us -> 80.6 us  [gather_rows(): pl.pallas_call(functools.partial(gather_kernel, whole), out_shape=jax.Sha...]
    all_gather x2 -> x0, blocking collectives: 58.3 us -> none  [the longest x1 31.5 us: small_device(): router_full = lax.all_gather(router_weight, 'fsdp', axis=0, tiled=True)]
    pallas_call x4 -> x3, Pallas kernels: 199 us -> 163 us  [sum_rows(): pl.pallas_call(functools.partial(sum_kernel, whole), out_shape=jax.ShapeD...]
    all_to_all x2 -> x0, waiting for transfers between devices: 24.6 us -> none  [fetch(): lax.all_to_all(cut, 'fsdp', split_axis=0, concat_axis=0, tiled=True)]
    all_to_all x2 -> x0, starting transfers between devices: 13 us -> none  [fetch(): lax.all_to_all(cut, 'fsdp', split_axis=0, concat_axis=0, tiled=True)]
  transfers between devices with their start and end apart: 8 -> 5, of which waited for: 3 -> 2; matrix products, arithmetic and copies ran while one was open for 6% -> 5% of each run, Pallas kernels for 36% -> 26%
where the time goes in v2:
time: 687 us; the launch traced here: 677 us
  Pallas kernels  486 us (71%)
  waiting for transfers between devices  58.1 us (8%)
  blocking collectives  47.3 us (7%)
  matrix products  24 us (3%)
  other arithmetic  19.5 us (3%)
  between operations  15.6 us (2%)
  local copies, waits for them, and re-layouts  15.5 us (2%)
  starting transfers between devices  10.7 us (2%)
    pallas_call x3, Pallas kernels, sum_rows(): pl.pallas_call(functools.partial(sum_kernel, whole), out_shape=jax.ShapeD...  163 us
    pallas_call x1, Pallas kernels, begin(): pl.pallas_call(functools.partial(begin_kernel, heads), out_shape=(shape(*...  144 us
    pallas_call x1, Pallas kernels, run_experts(): pl.pallas_call(functools.partial(experts_kernel, experts, ids.shape[1]),...  86.1 us
    pallas_call x2, Pallas kernels, gather_rows(): pl.pallas_call(functools.partial(gather_kernel, whole), out_shape=jax.Sha...  80.6 us
    reduce_scatter x2, waiting for transfers between devices, scattered(): return lax.psum_scatter(value, 'fsdp', scatter_dimension=0, tiled=True)  50.2 us
    unnamed x1, blocking collectives  29.4 us
  transfers between devices with their start and end apart: 5, of which 2 were waited for; matrix products, arithmetic and copies ran while one was open for 5% of the time, Pallas kernels for 26%

profile of v2, /device:TPU:16, one launch (start us, length us, event | category | flops | bytes accessed | tf_op | source)
XLA Modules:
  0.0 677.0 jit_solution(8186059177605518700)
XLA Ops:
  8.7 2.5 fusion.21.normed
  11.3 144.4 %begin.1 = (bf16[1,1024,2048]{2,1,0:T(8,128)(2,1)}, bf16[2048,512]{1,0:T(8,128)(2,1)}, bf16[2048,256]{1,0:T(8,128)(2,1)}, bf16[32,2048]{1,0:T(8,128)(2,1)}, s32[...) custom-call(bf16[2,128,2048]{2,1,0:T(8,128)(2,1)} %fusion.21.normed,, ...), custom_call_target="tpu_custom_call" | custom-call | tf_op jit(solution)/shard_map/begin/pallas_call | solution.py:761
  159.0 52.2 %gather_whole.1 = bf16[2,1024,2048]{2,1,0:T(8,128)(2,1)} custom-call(bf16[2,128,2048]{2,1,0:T(8,128)(2,1)} %multiply_convert_fusion.in_ref), custom_call_target="tpu_custom_call" | custom-call | tf_op jit(solution)/shard_map/gather_whole/pallas_call | solution.py:359
  213.7 86.1 %experts.1 = (bf16[2048,2048]{1,0:T(8,128)(2,1)}, bf16[2048,2048]{1,0:T(8,128)(2,1)}, f32[2048,128]{1,0:T(8,128)}, f32[768,2048]{1,0:T(8,128)}, f32[768,2048]{1,0:T(8,128)}, /*index=5*/f32[768,2048]{1,0:T(8,128)}) custom-call(s32[1]{0:T(128)} %bitcast.4.first_ref, bf16[2048,2048]{1,0:T(8,128)(2,1)} %bitcast.71, bf16[2048,2048]{1,0:T(8,128)(2,1)} %bitcast.74, ...), custom_call_target="tpu_custom_call" | custom-call | tf_op jit(solution)/shard_map/experts/pallas_call | solution.py:534
  299.9 2.2 copy.49
  302.2 57.6 %sum_whole.3 = bf16[2,128,2048]{2,1,0:T(8,128)(2,1)} custom-call(bf16[2,1024,2048]{2,1,0:T(8,128)(2,1)} %bitcast.73), custom_call_target="tpu_custom_call" | custom-call | tf_op jit(solution)/shard_map/sum_whole/pallas_call | solution.py:326
  360.3 7.9 %reduce-scatter.4.cloned.1.call-done = f32[2,128,32]{1,2,0:T(8,128)} async-done(((f32[2,1024,32]{1,2,0:T(8,128)}), f32[2,128,32]{1,2,0:T(8,128)}) %reduce-scatter.4.cloned.1.call-update) | async-done | bytes 32784 | tf_op jit(solution)/shard_map/reduce_scatter | solution.py:1317
  368.2 11.0 %psum.14 = f32[2,128,32]{1,2,0:T(8,128)S(1)} all-reduce(f32[2,128,32]{1,2,0:T(8,128)} %reduce-scatter.4.cloned.1.call-done), channel_id=1, replica_groups=mesh['fsdp'=8,'tp'=4] {'tp'}, use_global_device_ids=true, to_apply=%region_6.7 | all-reduce | flops 8192 | bytes 65536 | tf_op jit(solution)/shard_map/psum | solution.py:1316
  379.2 2.3 multiply_reduce_fusion
  384.8 28.4 %gather_half.1 = bf16[1,1024,2048]{2,1,0:T(8,128)(2,1)} custom-call(bf16[2,128,2048]{2,1,0:T(8,128)(2,1)} %fusion.33.in_ref), custom_call_target="tpu_custom_call" | custom-call | tf_op jit(solution)/shard_map/gather_half/pallas_call | solution.py:359
  413.1 4.6 fusion.14
  417.7 5.7 all-to-all-start.1
  423.4 4.5 fusion.26.dctx_ref
  428.0 12.0 %attend_back.1 = (bf16[1024,512]{1,0:T(8,128)(2,1)}, f32[2,128]{1,0:T(2,128)}) custom-call(bf16[1024,256]{1,0:T(8,128)(2,1)} %fusion.26.dctx_ref, f32[1024,384]{1,0:T(8,128)} %get-tuple-element.41.pre_ref, bf16[1024,512]{1,0:T(8,128)(2,1)} %get-tuple-element.42.qkv_ref, bf16[2,1024,1024]{2,1,0:T(8,128)(2,1)} %get-tuple-element.43.prob_ref, ...), custom_call_target="tpu_custom_call" | custom-call | tf_op jit(solution)/shard_map/attend_back/pallas_call | solution.py:443
  440.0 4.9 fusion.11
  448.2 62.0 %sum_whole.2 = bf16[2,128,2048]{2,1,0:T(8,128)(2,1)} custom-call(bf16[2,1024,2048]{2,1,0:T(8,128)(2,1)} %bitcast.72), custom_call_target="tpu_custom_call" | custom-call | tf_op jit(solution)/shard_map/sum_whole/pallas_call | solution.py:326
  510.2 4.8 all-to-all-start
  515.2 6.2 convert_bitcast_fusion.in_ref
  521.4 43.7 %sum_half.1 = bf16[2,128,2048]{2,1,0:T(8,128)(2,1)} custom-call(bf16[1,1024,2048]{2,1,0:T(8,128)(2,1)} %convert_bitcast_fusion.in_ref), custom_call_target="tpu_custom_call" | custom-call | tf_op jit(solution)/shard_map/sum_half/pallas_call | solution.py:326
  565.1 6.9 %psum.15 = f32[2,128]{1,0:T(2,128)S(1)} all-reduce(f32[2,128]{1,0:T(2,128)S(1)} %copy-done.10), channel_id=1, replica_groups=mesh['fsdp'=8,'tp'=4] {'tp'}, use_global_device_ids=true, to_apply=%region_12.13 | all-reduce | flops 256 | bytes 2048 | tf_op jit(solution)/shard_map/psum | solution.py:1355
  572.0 1.9 fusion.23
  573.9 29.4 %all-reduce.5 = (f32[2048]{0:T(1024)S(1)}, f32[128]{0:T(128)S(1)}, f32[128]{0:T(128)S(1)}, f32[2048]{0:T(1024)S(1)}) all-reduce(f32[2048]{0:T(1024)S(1)} %get-tuple-element.82, f32[128]{0:T(128)S(1)} %get-tuple-element.95, f32[128]{0:T(128)S(1)} %get-tuple-element.94, ...), channel_id=3, replica_groups=mesh['fsdp'=8,'tp'=4] {'fsdp'}, use_global_device_ids=true, to_apply=%region_11.12.clone | all-reduce | flops 4352 | bytes 34816
  606.8 5.4 fusion.20
  620.1 50.2 %reduce-scatter.8.cloned.1.call-done = f32[256,32]{0,1:T(8,128)} async-done(((f32[2048,32]{0,1:T(8,128)}), f32[256,32]{0,1:T(8,128)}) %reduce-scatter.8.cloned.1.call-update) | async-done | bytes 32784 | tf_op jit(solution)/shard_map/reduce_scatter | solution.py:1358
  (63 shorter events, 24.6 us)
Async XLA Ops:
  7.2 361.0 %reduce-scatter.4.cloned.1.call-start = ((), (), s32[]{:S(2)}) async-start(), calls=%async_computation.5 | async-start | bytes 294912 | tf_op jit(solution)/shard_map/reduce_scatter | solution.py:1317
  11.3 144.4 %copy-start = (bf16[2,128,2048]{2,1,0:T(8,128)(2,1)S(1)}, bf16[2,128,2048]{2,1,0:T(8,128)(2,1)}, u32[]{:S(2)}) copy-start(bf16[2,128,2048]{2,1,0:T(8,128)(2,1)} %param.17) | copy-start | bytes 3145732
  155.7 1.8 copy-start.1
  155.7 1.8 copy-start.6
  159.0 52.2 %copy-start.5 = (bf16[32,2048]{1,0:T(8,128)(2,1)S(1)}, bf16[32,2048]{1,0:T(8,128)(2,1)}, u32[]{:S(2)}) copy-start(bf16[32,2048]{1,0:T(8,128)(2,1)} %get-tuple-element.36) | copy-start | bytes 393220
  159.0 52.5 %copy-start.8 = (s32[2,8,1024]{2,1,0:T(8,128)S(1)}, s32[2,8,1024]{2,1,0:T(8,128)}, u32[]{:S(2)}) copy-start(s32[2,8,1024]{2,1,0:T(8,128)} %get-tuple-element.35) | copy-start | bytes 196612
  302.1 57.6 %copy-start.9 = (s32[2,128,8]{1,2,0:T(8,128)S(1)}, s32[2,128,8]{1,2,0:T(8,128)}, u32[]{:S(2)}) copy-start(s32[2,128,8]{1,2,0:T(8,128)} %param.19) | copy-start | bytes 24580
  302.2 57.7 %copy-start.3 = (bf16[2,128,2048]{2,1,0:T(8,128)(2,1)S(1)}, bf16[2,128,2048]{2,1,0:T(8,128)(2,1)}, u32[]{:S(2)}) copy-start(bf16[2,128,2048]{2,1,0:T(8,128)(2,1)} %multiply_convert_fusion.in_ref) | copy-start | bytes 3145732
  379.2 3.7 copy-start.4
  381.6 1.4 copy-start.2
  417.7 92.5 %all-to-all-start.1 = ((bf16[8,256,256]{2,1,0:T(8,128)(2,1)}), bf16[8,256,256]{2,1,0:T(8,128)(2,1)}, u32[]{:S(2)}, u32[]{:S(2)}) async-start(bf16[8,256,256]{2,1,0:T(8,128)(2,1)} %bitcast.86), calls=%async_computation.3 | async-start | bytes 2097152 | tf_op jit(solution)/shard_map/all_to_all | solution.py:1274
  423.4 195.0 %reduce-scatter.6.cloned.1.call-start = ((), (), s32[]{:S(2)}) async-start(), calls=%async_computation.6 | async-start | bytes 1179648 | tf_op jit(solution)/shard_map/reduce_scatter | solution.py:1358
  444.8 1.5 copy-start.11
  510.2 105.1 %all-to-all-start = ((bf16[8,256,256]{2,1,0:T(8,128)(2,1)}), bf16[8,256,256]{2,1,0:T(8,128)(2,1)}, u32[]{:S(2)}, u32[]{:S(2)}) async-start(bf16[8,256,256]{2,1,0:T(8,128)(2,1)} %bitcast.80), calls=%async_computation.1 | async-start | bytes 2097152 | tf_op jit(solution)/shard_map/all_to_all | solution.py:1274
  515.0 155.3 %reduce-scatter.8.cloned.1.call-start = ((), (), s32[]{:S(2)}) async-start(), calls=%async_computation.7 | async-start | bytes 294912 | tf_op jit(solution)/shard_map/reduce_scatter | solution.py:1358
  521.4 43.7 %copy-start.10 = (f32[2,128]{1,0:T(2,128)S(1)}, f32[2,128]{1,0:T(2,128)}, u32[]{:S(2)}) copy-start(f32[2,128]{1,0:T(2,128)} %get-tuple-element.46) | copy-start | bytes 3076
  521.4 50.6 %copy-start.7 = (f32[2048]{0:T(1024)S(1)}, f32[2048]{0:T(1024)}, u32[]{:S(2)}) copy-start(f32[2048]{0:T(1024)} %param.20) | copy-start | bytes 24580
Sparse Core Ops, SparseCore 0:
  302.3 65.8 reduce-scatter.3
  446.5 63.6 reduce-scatter.5
  606.9 63.2 reduce-scatter.7
